TPU v7x, 256 devices: a whole 4x4x8 slice. The times are simulated.
256 devices in a mesh: example: 32 (over y, z_hi, core), layer: 8 (over z_lo, x).
Axes of the slice: x: 4, y: 4, z: 8 (z_hi: 4, z_lo: 2; z = z_hi * 2 + z_lo), core: 2. Of those that a mesh axis runs over, the one named last changes fastest.
Arguments:
- query_grads: bfloat16 [8, 1024, 4096], P('layer', 'example'), may hold values from -6 to 6
- doc_grads: bfloat16 [8, 16384, 4096], P('layer', 'example'), may hold values from -0.14941406 to 0.14941406
- out_basis: float32 [8, 32, 32], P('layer', 'example'), may hold values from -1 to 1
- in_basis: float32 [8, 128, 128], P('layer', 'example'), may hold values from -0.5 to 0.5
- eigenvalues: float32 [8, 32, 128], P('layer', 'example'), may hold values from 0.5 to 16
- damping: float32 [8], P('layer'), may hold values from 0.1 to 1
Outputs:
- scores: float32 [1024, 16384], P('layer', 'example')
All inputs are finite; a program needn't handle non-finite values.
Results may differ from a plain program's by a relative error of at most 0.0029.
Values may be sent and summed in bfloat16 or wider, within the bound.
No kernel may reach another device: no remote copies, remote signals or barrier semaphores. Data moves between devices by JAX's collectives and lax.ppermute only.
A program may use at most 128 MiB of HBM per device.

v0:
```python
import functools
import jax
import jax.numpy as jnp
from jax import lax
from jax.experimental import pallas as pl
from jax.experimental.pallas import tpu as pltpu
from jax.sharding import PartitionSpec as P

NY, NZ, NC = 4, 4, 2
NL, NX = 2, 4
ROWS = 32
CHUNK = 8
OUT, IN = 32, 128
F32, BF16 = jnp.float32, jnp.bfloat16
VMEM = pl.BlockSpec(memory_space=pltpu.VMEM)
SMEM = pl.BlockSpec(memory_space=pltpu.SMEM)
ANY = pl.BlockSpec(memory_space=pl.ANY)
HBM = pl.BlockSpec(memory_space=pltpu.HBM)


def example_shift(dy, dz, dc):
    def place(y, z, c):
        return (y % NY) * NZ * NC + (z % NZ) * NC + c % NC

    return [
        (place(y, z, c), place(y + dy, z + dz, c + dc))
        for y in range(NY)
        for z in range(NZ)
        for c in range(NC)
    ]


def layer_shift(dl, dx):
    return [
        (a * NX + x, ((a + dl) % NL) * NX + (x + dx) % NX) for a in range(NL) for x in range(NX)
    ]


def send(x, dy=0, dz=0, dc=0):
    return lax.ppermute(x, "example", example_shift(dy, dz, dc))


def split2(x):
    high = x.astype(BF16)
    return high, (x - high.astype(F32)).astype(BF16)


def mm(a, b, contract=((1,), (0,))):
    return lax.dot_general(a, b, (contract, ((), ())), preferred_element_type=F32)


def coordinates(example):
    return example >> 3, (example >> 1) & 3, example & 1


def held_kernel(x_ref, *refs):
    pltpu.sync_copy(x_ref, refs[-1])


def held(x, after=()):
    return pl.pallas_call(
        held_kernel,
        out_shape=jax.ShapeDtypeStruct(x.shape, x.dtype),
        in_specs=[HBM] + [ANY] * len(after),
        out_specs=VMEM,
        compiler_params=pltpu.CompilerParams(vmem_limit_bytes=16 << 20),
        cost_estimate=pl.CostEstimate(flops=0, bytes_accessed=2 * x.nbytes, transcendentals=0),
        name="held",
    )(x, *after)


def pack_kernel(in_ref, eig_ref, basis_ref, out_ref, in_rows, eig_rows, basis_rows, sems):
    copies = [
        pltpu.make_async_copy(source, target, sems.at[k])
        for k, (source, target) in enumerate(
            ((in_ref, in_rows), (eig_ref, eig_rows), (basis_ref, basis_rows))
        )
    ]
    for copy in copies:
        copy.start()
    out_ref[...] = jnp.zeros_like(out_ref)
    for copy in copies:
        copy.wait()
    out_ref[0:4, :] = in_rows[...]
    out_ref[4:5, :] = eig_rows[...]
    out_ref[5:6, 0:OUT] = basis_rows[...]


def pack(*parts):
    return pl.pallas_call(
        pack_kernel,
        out_shape=jax.ShapeDtypeStruct((8, IN), F32),
        in_specs=[HBM] * 3,
        out_specs=VMEM,
        scratch_shapes=[pltpu.VMEM(p.shape, p.dtype) for p in parts]
        + [pltpu.SemaphoreType.DMA((3,))],
        compiler_params=pltpu.CompilerParams(vmem_limit_bytes=1 << 20),
        name="pack",
    )(*parts)


def join_kernel(ranges, *refs):
    out_ref, at = refs[-1], 0
    for part, (low, high) in zip(refs, ranges):
        out_ref[at : at + high - low, :] = part[low:high, :]
        at += high - low


def join(parts, after, ranges=None):
    ranges = ranges or [(0, p.shape[0]) for p in parts]
    rows = sum(high - low for low, high in ranges)
    columns, dtype = parts[0].shape[1], parts[0].dtype
    return pl.pallas_call(
        functools.partial(join_kernel, ranges),
        out_shape=jax.ShapeDtypeStruct((rows, columns), dtype),
        in_specs=[VMEM] * len(parts) + [ANY] * len(after),
        out_specs=VMEM,
        compiler_params=pltpu.CompilerParams(vmem_limit_bytes=8 << 20),
        name="join",
    )(*parts, *after)


def prepare_kernel(place_ref, damp_ref, *refs):
    pieces, rows = refs[:NZ], refs[-1]
    left_ref, right_ref, in_ref, back_ref, scale_ref = refs[-6:-1]
    y, z, c = coordinates(place_ref[0])
    for dz in range(NZ):
        for dy in range(NY):
            for dc in range(NC):
                owner = ((y - dy) & 3) * 8 + ((z - dz) & 3) * 2 + (c ^ dc)
                k = dy * NC + dc
                piece = pieces[dz][8 * k : 8 * k + 8, :]
                rows[pl.ds(pl.multiple_of(owner * 8, 8), 8), :] = piece
    table = rows[...]
    high, low = split2(table)
    lowest = (table - high.astype(F32) - low.astype(F32)).astype(BF16)

    def iota(shape, axis):
        return lax.broadcasted_iota(jnp.int32, shape, axis)

    def pick(condition):
        return condition.astype(F32).astype(BF16)

    r, k = iota((IN, 256), 0), iota((IN, 256), 1)
    pick_in = pick(k == (r // 4) * 8 + r % 4)
    basis, rest = mm(pick_in, high), mm(pick_in, low)
    in_ref[...] = jnp.concatenate([basis, rest], axis=0).astype(BF16)
    turned, turned_rest = basis.T, rest.T
    back_ref[...] = jnp.concatenate(
        [
            jnp.concatenate([turned, turned_rest], axis=1),
            jnp.concatenate([turned, jnp.zeros_like(turned)], axis=1),
        ],
        axis=0,
    ).astype(BF16)
    r, k = iota((256, 256), 0), iota((256, 256), 1)
    pick_eig = pick(k == (r // 8) * 8 + 4)
    eig = mm(pick_eig, high) + (mm(pick_eig, low) + mm(pick_eig, lowest))
    scale_ref[...] = 1.0 / (eig + damp_ref[0])
    pick_out = pick(k == (r // 8) * 8 + 5)
    spread = pick(iota((IN, 256), 0) == iota((IN, 256), 1) // 8)
    same = (r % 8 == k % 8).astype(F32)
    for term, part in enumerate((high, low)):
        whole = mm(mm(pick_out, part).astype(BF16), spread) * same
        right_ref[256 * term : 256 * (term + 1), :] = whole.astype(BF16)
        left_ref[256 * term : 256 * (term + 1), :] = whole.T.astype(BF16)


def prepare(place, damping, pieces, after):
    shape = jax.ShapeDtypeStruct
    return pl.pallas_call(
        prepare_kernel,
        out_shape=(
            shape((512, 256), BF16),
            shape((512, 256), BF16),
            shape((2 * IN, IN), BF16),
            shape((2 * IN, 2 * IN), BF16),
            shape((256, IN), F32),
        ),
        in_specs=[SMEM, SMEM] + [VMEM] * NZ + [ANY] * len(after),
        out_specs=(VMEM,) * 5,
        scratch_shapes=[pltpu.VMEM((256, 128), F32)],
        compiler_params=pltpu.CompilerParams(vmem_limit_bytes=16 << 20),
        cost_estimate=pl.CostEstimate(flops=200_000_000, bytes_accessed=1 << 20, transcendentals=0),
        name="prepare",
    )(place, damping, *pieces, *after)


def mix(matrix, x):
    high, low = split2(x)
    both = mm(matrix, high)
    return both[:256] + (both[256:] + mm(matrix[:256], low))


def rotate_chunk(x, left, right, basis, back, scale):
    count = 2 * len(x)
    tall = jnp.concatenate(
        [piece[:, IN * i : IN * (i + 1)] for piece in x for i in range(OUT)], axis=0
    )
    half = mm(jnp.concatenate([tall, tall], axis=1), basis)
    half = half.reshape(count // 2, OUT, 2, 8, IN)
    side = jnp.concatenate(
        [half[g // 2, :, g % 2].reshape(OUT * 8, IN) for g in range(count)], axis=1
    )
    rotated = mix(left, side)
    scaled = jnp.concatenate(
        [rotated[:, IN * g : IN * (g + 1)] * scale for g in range(count)], axis=0
    )
    restored = mm(jnp.concatenate(split2(scaled), axis=1), back)
    restored = restored[:, :IN] + restored[:, IN:]
    side = jnp.concatenate([restored[256 * g : 256 * (g + 1)] for g in range(count)], axis=1)
    return mix(right, side)


def rotate_kernel(most, count, left_ref, right_ref, in_ref, back_ref, scale_ref, *refs):
    blocks, out_ref = refs[:count], refs[-1]
    pieces = [(b, at) for b in blocks for at in range(0, b.shape[0], 16)]
    step = -(-len(pieces) // -(-len(pieces) // most))
    for first in range(0, len(pieces), step):
        chunk = pieces[first : first + step]
        done = rotate_chunk(
            [b[at : at + 16, :] for b, at in chunk],
            left_ref[...],
            right_ref[...],
            in_ref[...],
            back_ref[...],
            scale_ref[...],
        )
        for p in range(len(chunk)):
            to = 16 * (first + p)
            for i in range(OUT):
                rows = done[8 * i : 8 * i + 8, 2 * IN * p : 2 * IN * (p + 1)]
                rows = jnp.concatenate([rows[:, :IN], rows[:, IN:]], axis=0)
                out_ref[to : to + 16, IN * i : IN * (i + 1)] = rows.astype(BF16)


def rotate(tables, blocks, after, flops=0):
    rows = sum(b.shape[0] for b in blocks)
    width = blocks[0].shape[1]
    return pl.pallas_call(
        functools.partial(rotate_kernel, CHUNK, len(blocks)),
        out_shape=jax.ShapeDtypeStruct((rows, width), BF16),
        in_specs=[VMEM] * (5 + len(blocks)) + [ANY] * len(after),
        out_specs=VMEM,
        compiler_params=pltpu.CompilerParams(vmem_limit_bytes=32 << 20),
        cost_estimate=pl.CostEstimate(flops=flops, bytes_accessed=0, transcendentals=0),
        name="rotate",
    )(*tables, *blocks, *after)


def scores_of(conditioned, documents):
    return lax.dot_general(
        conditioned, documents, (((1,), (1,)), ((), ())), preferred_element_type=F32
    ).astype(BF16)


def arrange_kernel(offsets, place_ref, *refs):
    parts, out_ref = refs[: 2 * len(offsets)], refs[-1]
    y, z, c = coordinates(place_ref[0])
    layer = place_ref[1]
    for k, part in enumerate(parts):
        kind = c ^ (k % 2)
        for at, (dy, dz) in enumerate(offsets[k // 2]):
            from_z = (z - dz) & 3
            to = ((y - dy) & 3) * 2 + (from_z >> 1)
            turn = ((to ^ layer) & 4) + ((to - layer) & 3)
            out_ref[turn * 4 + (from_z & 1) * 2 + kind] = part[ROWS * at : ROWS * (at + 1), :]


def arrange(place, offsets, parts, after):
    count = sum(p.shape[0] for p in parts) // ROWS
    columns = parts[0].shape[1]
    return pl.pallas_call(
        functools.partial(arrange_kernel, offsets),
        out_shape=jax.ShapeDtypeStruct((count, ROWS, columns), BF16),
        in_specs=[SMEM] + [VMEM] * len(parts) + [ANY] * len(after),
        out_specs=VMEM,
        compiler_params=pltpu.CompilerParams(vmem_limit_bytes=16 << 20),
        cost_estimate=pl.CostEstimate(
            flops=0, bytes_accessed=count * ROWS * columns * 4, transcendentals=0
        ),
        name="arrange",
    )(place, *parts, *after)


def finish_kernel(*refs):
    total = refs[0][...].astype(F32)
    for part in refs[1:-1]:
        total += part[...].astype(F32)
    refs[-1][...] = total


def finish(parts):
    return pl.pallas_call(
        finish_kernel,
        out_shape=jax.ShapeDtypeStruct(parts[0].shape, F32),
        in_specs=[VMEM] * len(parts),
        out_specs=VMEM,
        compiler_params=pltpu.CompilerParams(vmem_limit_bytes=8 << 20),
        name="finish",
    )(*parts)


def spread_over_layers(ready):
    ready = ready.reshape(NL * NX, 4 * ROWS, ready.shape[-1])
    parts = [ready[0]]
    for dl, dx in ((1, 2), (0, 2), (1, 1), (1, 3), (1, 0), (0, 1), (0, 3)):
        parts.append(lax.ppermute(ready[dl * NX + dx], "layer", layer_shift(dl, dx)))
    return parts


def halves_kernel(behind_ref, ahead_ref, *refs):
    first_ref, second_ref = refs[-2:]
    rows = first_ref.shape[0]
    first_ref[...] = behind_ref[:rows, :]
    second_ref[...] = ahead_ref[rows:, :]


def halves(behind, ahead, after):
    rows, columns = behind.shape
    return pl.pallas_call(
        halves_kernel,
        out_shape=(jax.ShapeDtypeStruct((rows // 2, columns), behind.dtype),) * 2,
        in_specs=[VMEM, VMEM] + [ANY] * len(after),
        out_specs=(VMEM, VMEM),
        compiler_params=pltpu.CompilerParams(vmem_limit_bytes=4 << 20),
        name="halves",
    )(behind, ahead, *after)


def both_ways(own, axis):
    return send(own, **{axis: 1}), send(own, **{axis: -1})


def body(query_grads, doc_grads, out_basis, in_basis, eigenvalues, damping):
    place = jnp.stack([lax.axis_index("example"), lax.axis_index("layer")])

    own, docs = query_grads[0], doc_grads[0]
    docs_there = send(docs, dc=1)

    near = both_ways(own, "dz")
    row = pack(in_basis[0], eigenvalues[0], out_basis[0])
    pair = join([row, send(row, dc=1)], [])
    column = [send(pair, dy=d) for d in range(1, NY)]
    plane = join([pair] + column, [docs_there])
    pieces = [plane] + [send(plane, dz=d) for d in range(1, NZ)]
    tables = prepare(place, damping, pieces, [])

    cut = halves(*near, pieces[1:3])
    far = send(cut[0], dz=1), send(cut[1], dz=-1)

    side = rotate(tables, (own, *near), [cut[0]])
    side_y = both_ways(side, "dy")
    other = rotate(tables, far, [side], 20_000_000_000)
    other_y = both_ways(other, "dy")

    low = join([side_y[1]], [], [(ROWS, 3 * ROWS)])
    high = join([side_y[0], other_y[0]], [], [(0, ROWS), (0, ROWS)])
    side_far = send(high, dy=1), send(low, dy=-1)

    docs_other = held(docs_there, [other])

    offsets = [
        [(0, 0), (0, 1), (0, -1), (0, 2)],
        [(1, 0), (1, 1), (1, -1), (-1, 0), (-1, 1), (-1, -1), (1, 2), (-1, 2)],
        [(2, 0), (2, 2), (2, 1), (2, -1)],
    ]
    parts = []
    for blocks, after in (((side, other), [docs_other]), ((*side_y, *other_y), [high, low]), (side_far, [])):
        conditioned = join(blocks, after + parts[-2:-1])
        theirs = send(scores_of(conditioned, docs_other), dc=1)
        parts += [scores_of(conditioned, docs), theirs]
    return finish(spread_over_layers(arrange(place, offsets, parts, [])))


def solution(mesh):
    placed = P("layer", "example", None)
    return jax.shard_map(
        body,
        mesh=mesh,
        in_specs=(placed,) * 5 + (P("layer"),),
        out_specs=P("layer", "example"),
        check_vma=False,
    )
```

profile of v0, /device:TPU:24, one launch (start us, length us, event | category | flops | bytes accessed | tf_op | source)
XLA Modules:
  0.0 97.6 jit_solution(6232708315260280190)
XLA Ops:
  0.0 0.0 collective-permute-start.4
  0.0 3.3 %collective-permute-start.8 = (bf16[32,4096]{1,0:T(8,128)(2,1)}, bf16[32,4096]{1,0:T(8,128)(2,1)S(1)}, u32[]{:S(2)}, u32[]{:S(2)}) collective-permute-start(bf16[32,4096]{1,0:T(8,128)(2,1)} %bitcast.31), channel_id=1, source_target_pairs={{0,16},{8,24},{16,32},{24,40},{32,48},{40,56},{48,0},{56,8},{64,80... | collective-permute-start | bytes 786440 | tf_op jit(solution)/shard_map/ppermute | solution.py:40
  3.4 3.1 %collective-permute-start.9 = (bf16[32,4096]{1,0:T(8,128)(2,1)}, bf16[32,4096]{1,0:T(8,128)(2,1)S(1)}, u32[]{:S(2)}, u32[]{:S(2)}) collective-permute-start(bf16[32,4096]{1,0:T(8,128)(2,1)} %bitcast.32), channel_id=1, source_target_pairs={{0,48},{8,56},{16,0},{24,8},{32,16},{40,24},{48,32},{56,40},{64,11... | collective-permute-start | bytes 786440 | tf_op jit(solution)/shard_map/ppermute | solution.py:40
  6.5 0.7 copy-done.3
  7.2 0.7 copy-done.4
  7.8 0.7 copy-done.5
  8.5 0.2 collective-permute-start
  8.7 1.1 %collective-permute-done.refs_1_ = f32[8,128]{1,0:T(8,128)S(1)} collective-permute-done((f32[8,128]{1,0:T(8,128)S(1)}, f32[8,128]{1,0:T(8,128)S(1)}, u32[]{:S(2)}, u32[]{:S(2)}) %collective-permute-start) | collective-permute-done | bytes 4128 | tf_op jit(solution)/shard_map/ppermute | solution.py:40
  9.8 0.2 collective-permute-start.1
  10.0 2.6 %collective-permute-start.2 = (f32[16,128]{1,0:T(8,128)S(1)}, f32[16,128]{1,0:T(8,128)S(1)}, u32[]{:S(2)}, u32[]{:S(2)}) collective-permute-start(f32[16,128]{1,0:T(8,128)S(1)} %join.7.refs_0_), channel_id=1, source_target_pairs={{0,128},{8,136},{16,144},{24,152},{32,160},{40,168},{48,176},{56,1... | collective-permute-start | bytes 24584 | tf_op jit(solution)/shard_map/ppermute | solution.py:40
  12.6 0.8 collective-permute-done.1.refs_1_
  13.4 0.7 collective-permute-start.3
  14.2 1.0 %collective-permute-done.2.refs_2_ = f32[16,128]{1,0:T(8,128)S(1)} collective-permute-done((f32[16,128]{1,0:T(8,128)S(1)}, f32[16,128]{1,0:T(8,128)S(1)}, u32[]{:S(2)}, u32[]{:S(2)}) %collective-permute-start.2) | collective-permute-done | bytes 8224 | tf_op jit(solution)/shard_map/ppermute | solution.py:40
  15.1 3.1 %collective-permute-done.3.refs_3_ = f32[16,128]{1,0:T(8,128)S(1)} collective-permute-done((f32[16,128]{1,0:T(8,128)S(1)}, f32[16,128]{1,0:T(8,128)S(1)}, u32[]{:S(2)}, u32[]{:S(2)}) %collective-permute-start.3) | collective-permute-done | bytes 8224 | tf_op jit(solution)/shard_map/ppermute | solution.py:40
  18.3 2.0 %copy-done = bf16[512,4096]{1,0:T(8,128)(2,1)} copy-done((bf16[512,4096]{1,0:T(8,128)(2,1)}, bf16[512,4096]{1,0:T(8,128)(2,1)S(1)}, u32[]{:S(2)}) %copy-start) | copy-done | bytes 4194328
  20.3 1.4 %collective-permute-start.5 = (f32[64,128]{1,0:T(8,128)S(1)}, f32[64,128]{1,0:T(8,128)S(1)}, u32[]{:S(2)}, u32[]{:S(2)}) collective-permute-start(f32[64,128]{1,0:T(8,128)S(1)} %join.8.refs_0_), channel_id=1, source_target_pairs={{0,16},{8,24},{16,32},{24,40},{32,48},{40,56},{48,0},{56,8},{64,80... | collective-permute-start | bytes 98312 | tf_op jit(solution)/shard_map/ppermute | solution.py:40
  21.6 4.7 %collective-permute-start.6 = (f32[64,128]{1,0:T(8,128)S(1)}, f32[64,128]{1,0:T(8,128)S(1)}, u32[]{:S(2)}, u32[]{:S(2)}) collective-permute-start(f32[64,128]{1,0:T(8,128)S(1)} %join.8.refs_0_), channel_id=1, source_target_pairs={{0,32},{8,40},{16,48},{24,56},{32,0},{40,8},{48,16},{56,24},{64,96... | collective-permute-start | bytes 98312 | tf_op jit(solution)/shard_map/ppermute | solution.py:40
  26.3 3.0 %collective-permute-start.7 = (f32[64,128]{1,0:T(8,128)S(1)}, f32[64,128]{1,0:T(8,128)S(1)}, u32[]{:S(2)}, u32[]{:S(2)}) collective-permute-start(f32[64,128]{1,0:T(8,128)S(1)} %join.8.refs_0_), channel_id=1, source_target_pairs={{0,48},{8,56},{16,0},{24,8},{32,16},{40,24},{48,32},{56,40},{64,11... | collective-permute-start | bytes 98312 | tf_op jit(solution)/shard_map/ppermute | solution.py:40
  29.3 0.0 collective-permute-done.8.behind_ref.refs_1_
  29.3 0.1 collective-permute-done.6.refs_2_.refs_1_
  29.5 4.2 %collective-permute-start.10 = (bf16[16,4096]{1,0:T(8,128)(2,1)S(1)}, bf16[16,4096]{1,0:T(8,128)(2,1)S(1)}, u32[]{:S(2)}, u32[]{:S(2)}) collective-permute-start(bf16[16,4096]{1,0:T(8,128)(2,1)S(1)} %get-tuple-element.17.refs_3_), channel_id=1, source_target_pairs={{0,16},{8,24},{16,32},{24,40},{32,48},{40,56},{48,0},{56,8},{64,80... | collective-permute-start | bytes 393224 | tf_op jit(solution)/shard_map/ppermute | solution.py:40
  33.7 0.0 collective-permute-start.11
  33.7 0.1 pad_add_fusion.place_ref
  34.4 1.2 %prepare.1 = (bf16[512,256]{1,0:T(8,128)(2,1)S(1)}, bf16[512,256]{1,0:T(8,128)(2,1)S(1)}, bf16[256,128]{1,0:T(8,128)(2,1)S(1)}, bf16[256,256]{1,0:T(8,128)(2,1)S(1)}, f32[256,128]{1,0:T(8,128)S(1)}) custom-call(s32[2]{0:T(128)S(1)} %pad_add_fusion.place_ref, f32[1]{0:T(128)S(6)} %copy.7.damp_ref, f32[64,128]{1,0:T(8,128)S(1)} %join.8.refs_0_, ...), custom_call_target="tpu_custom_call" | custom-call | flops 200000000 | bytes 1048576 | tf_op jit(solution)/shard_map/prepare/pallas_call | solution.py:171
  35.6 2.6 %rotate.2.refs_2_.refs_0_ = bf16[96,4096]{1,0:T(8,128)(2,1)S(1)} custom-call(bf16[512,256]{1,0:T(8,128)(2,1)S(1)} %get-tuple-element.12.left_ref, bf16[512,256]{1,0:T(8,128)(2,1)S(1)} %get-tuple-element.13.right_ref, bf16[256,128]{1,0:T(8,128)(2,1)S(1)} %get-tuple-element.14.in_ref, bf16[256,256]{1,0:T(8,128)(2,1)S(1)} %get-tuple-element.15.back_ref, ...), custom_call_target="tpu_custom_call" | custom-call | tf_op jit(solution)/shard_map/rotate/pallas_call | solution.py:240
  38.2 0.3 collective-permute-start.13
  38.5 1.8 %collective-permute-start.14 = (bf16[96,4096]{1,0:T(8,128)(2,1)S(1)}, bf16[96,4096]{1,0:T(8,128)(2,1)S(1)}, u32[]{:S(2)}, u32[]{:S(2)}) collective-permute-start(bf16[96,4096]{1,0:T(8,128)(2,1)S(1)} %rotate.2.refs_2_.refs_0_), channel_id=1, source_target_pairs={{0,192},{8,200},{16,208},{24,216},{32,224},{40,232},{48,240},{56,2... | collective-permute-start | bytes 2359304 | tf_op jit(solution)/shard_map/ppermute | solution.py:40
  40.3 0.2 collective-permute-done.11.refs_1_
  40.6 1.4 %rotate.3.refs_0_.refs_1_ = bf16[32,4096]{1,0:T(8,128)(2,1)S(1)} custom-call(bf16[512,256]{1,0:T(8,128)(2,1)S(1)} %get-tuple-element.12.left_ref, bf16[512,256]{1,0:T(8,128)(2,1)S(1)} %get-tuple-element.13.right_ref, bf16[256,128]{1,0:T(8,128)(2,1)S(1)} %get-tuple-element.14.in_ref, bf16[256,256]{1,0:T(8,128)(2,1)S(1)} %get-tuple-element.15.back_ref, ...), custom_call_target="tpu_custom_call" | custom-call | flops 20000000000 | tf_op jit(solution)/shard_map/rotate/pallas_call | solution.py:240
  42.0 1.3 %collective-permute-start.15 = (bf16[32,4096]{1,0:T(8,128)(2,1)S(1)}, bf16[32,4096]{1,0:T(8,128)(2,1)S(1)}, u32[]{:S(2)}, u32[]{:S(2)}) collective-permute-start(bf16[32,4096]{1,0:T(8,128)(2,1)S(1)} %rotate.3.refs_0_.refs_1_), channel_id=1, source_target_pairs={{0,64},{8,72},{16,80},{24,88},{32,96},{40,104},{48,112},{56,120},{... | collective-permute-start | bytes 786440 | tf_op jit(solution)/shard_map/ppermute | solution.py:40
  43.3 0.8 collective-permute-start.16
  44.1 0.3 held.1.refs_2_
  44.4 0.1 join.9
  44.4 0.0 copy-start.6
  44.4 1.6 %convolution_convert_fusion.4 = bf16[128,512]{1,0:T(8,128)(2,1)S(1)} fusion(bf16[128,4096]{1,0:T(8,128)(2,1)S(1)} %join.9, bf16[512,4096]{1,0:T(8,128)(2,1)S(1)} %held.1.refs_2_), kind=kOutput, calls=%fused_computation.4 | convolution fusion | flops 536936448 | bytes 5373952 | tf_op jit(solution)/shard_map/dot_general | solution.py:252
  46.0 0.1 collective-permute-start.12
  46.1 0.5 copy-done.6
  46.6 1.5 %convolution_convert_fusion.5.refs_6_.refs_0_ = bf16[128,512]{1,0:T(8,128)(2,1)S(1)} fusion(bf16[128,4096]{1,0:T(8,128)(2,1)S(1)} %join.9, bf16[1,512,4096]{2,1,0:T(8,128)(2,1)S(1)} %copy-done.6), kind=kOutput, calls=%fused_computation.5 | convolution fusion | flops 536936448 | bytes 5373952 | tf_op jit(solution)/shard_map/dot_general | solution.py:252
  48.2 13.4 %collective-permute-done.15.refs_1_.refs_2_ = bf16[32,4096]{1,0:T(8,128)(2,1)S(1)} collective-permute-done((bf16[32,4096]{1,0:T(8,128)(2,1)S(1)}, bf16[32,4096]{1,0:T(8,128)(2,1)S(1)}, u32[]{:S(2)}, u32[]{:S(2)}) %collective-permute-start.15) | collective-permute-done | bytes 262176 | tf_op jit(solution)/shard_map/ppermute | solution.py:40
  61.6 0.4 collective-permute-start.18
  62.0 1.8 %collective-permute-start.19 = (bf16[64,4096]{1,0:T(8,128)(2,1)S(1)}, bf16[64,4096]{1,0:T(8,128)(2,1)S(1)}, u32[]{:S(2)}, u32[]{:S(2)}) collective-permute-start(bf16[64,4096]{1,0:T(8,128)(2,1)S(1)} %join.11.refs_5_), channel_id=1, source_target_pairs={{0,192},{8,200},{16,208},{24,216},{32,224},{40,232},{48,240},{56,2... | collective-permute-start | bytes 1572872 | tf_op jit(solution)/shard_map/ppermute | solution.py:40
  63.8 0.1 join.12
  63.9 1.3 %convolution_convert_fusion = bf16[256,512]{1,0:T(8,128)(2,1)S(1)} fusion(bf16[256,4096]{1,0:T(8,128)(2,1)S(1)} %join.12, bf16[512,4096]{1,0:T(8,128)(2,1)S(1)} %held.1.refs_2_), kind=kOutput, calls=%fused_computation | convolution fusion | flops 1073872896 | bytes 6553600 | tf_op jit(solution)/shard_map/dot_general | solution.py:252
  65.2 0.1 collective-permute-start.17
  65.3 1.3 %convolution_convert_fusion.1.refs_2_ = bf16[256,512]{1,0:T(8,128)(2,1)S(1)} fusion(bf16[256,4096]{1,0:T(8,128)(2,1)S(1)} %join.12, bf16[1,512,4096]{2,1,0:T(8,128)(2,1)S(1)} %copy-done.6), kind=kOutput, calls=%fused_computation.1 | convolution fusion | flops 1073872896 | bytes 6553600 | tf_op jit(solution)/shard_map/dot_general | solution.py:252
  66.6 5.0 %collective-permute-done.18.refs_0_ = bf16[64,4096]{1,0:T(8,128)(2,1)S(1)} collective-permute-done((bf16[64,4096]{1,0:T(8,128)(2,1)S(1)}, bf16[64,4096]{1,0:T(8,128)(2,1)S(1)}, u32[]{:S(2)}, u32[]{:S(2)}) %collective-permute-start.18) | collective-permute-done | bytes 524320 | tf_op jit(solution)/shard_map/ppermute | solution.py:40
  71.6 1.5 %collective-permute-done.19.refs_1_ = bf16[64,4096]{1,0:T(8,128)(2,1)S(1)} collective-permute-done((bf16[64,4096]{1,0:T(8,128)(2,1)S(1)}, bf16[64,4096]{1,0:T(8,128)(2,1)S(1)}, u32[]{:S(2)}, u32[]{:S(2)}) %collective-permute-start.19) | collective-permute-done | bytes 524320 | tf_op jit(solution)/shard_map/ppermute | solution.py:40
  73.1 0.1 join.13
  73.1 1.6 %convolution_convert_fusion.2 = bf16[128,512]{1,0:T(8,128)(2,1)S(1)} fusion(bf16[128,4096]{1,0:T(8,128)(2,1)S(1)} %join.13, bf16[512,4096]{1,0:T(8,128)(2,1)S(1)} %held.1.refs_2_), kind=kOutput, calls=%fused_computation.2 | convolution fusion | flops 536936448 | bytes 5373952 | tf_op jit(solution)/shard_map/dot_general | solution.py:252
  74.7 0.3 collective-permute-start.20
  75.0 1.5 %convolution_convert_fusion.3.refs_4_ = bf16[128,512]{1,0:T(8,128)(2,1)S(1)} fusion(bf16[128,4096]{1,0:T(8,128)(2,1)S(1)} %join.13, bf16[1,512,4096]{2,1,0:T(8,128)(2,1)S(1)} %copy-done.6), kind=kOutput, calls=%fused_computation.3 | convolution fusion | flops 536936448 | bytes 5373952 | tf_op jit(solution)/shard_map/dot_general | solution.py:252
  76.6 0.7 arrange.1
  77.3 0.1 fusion.3
  77.4 3.8 %collective-permute-start.21 = (bf16[128,512]{1,0:T(8,128)(2,1)S(1)}, bf16[128,512]{1,0:T(8,128)(2,1)S(1)}, u32[]{:S(2)}, u32[]{:S(2)}) collective-permute-start(bf16[128,512]{1,0:T(8,128)(2,1)S(1)} %bitcast.44), channel_id=1, source_target_pairs={{0,6},{1,7},{2,4},{3,5},{4,2},{5,3},{6,0},{7,1},{8,14},{9,15},{10,... | collective-permute-start | bytes 393224 | tf_op jit(solution)/shard_map/ppermute | solution.py:308
  81.2 0.5 collective-permute-start.22
  81.7 1.7 %collective-permute-start.23 = (bf16[128,512]{1,0:T(8,128)(2,1)S(1)}, bf16[128,512]{1,0:T(8,128)(2,1)S(1)}, u32[]{:S(2)}, u32[]{:S(2)}) collective-permute-start(bf16[128,512]{1,0:T(8,128)(2,1)S(1)} %bitcast.42), channel_id=1, source_target_pairs={{0,5},{1,6},{2,7},{3,4},{4,1},{5,2},{6,3},{7,0},{8,13},{9,14},{10,... | collective-permute-start | bytes 393224 | tf_op jit(solution)/shard_map/ppermute | solution.py:308
  83.4 2.4 %collective-permute-start.24 = (bf16[128,512]{1,0:T(8,128)(2,1)S(1)}, bf16[128,512]{1,0:T(8,128)(2,1)S(1)}, u32[]{:S(2)}, u32[]{:S(2)}) collective-permute-start(bf16[128,512]{1,0:T(8,128)(2,1)S(1)} %bitcast.41), channel_id=1, source_target_pairs={{0,7},{1,4},{2,5},{3,6},{4,3},{5,0},{6,1},{7,2},{8,15},{9,12},{10,... | collective-permute-start | bytes 393224 | tf_op jit(solution)/shard_map/ppermute | solution.py:308
  85.8 0.8 collective-permute-start.25
  86.6 0.8 collective-permute-start.26
  87.4 4.5 %collective-permute-done.22.refs_2_ = bf16[128,512]{1,0:T(8,128)(2,1)S(1)} collective-permute-done((bf16[128,512]{1,0:T(8,128)(2,1)S(1)}, bf16[128,512]{1,0:T(8,128)(2,1)S(1)}, u32[]{:S(2)}, u32[]{:S(2)}) %collective-permute-start.22) | collective-permute-done | bytes 131104 | tf_op jit(solution)/shard_map/ppermute | solution.py:308
  91.8 1.4 %collective-permute-done.24.refs_4_ = bf16[128,512]{1,0:T(8,128)(2,1)S(1)} collective-permute-done((bf16[128,512]{1,0:T(8,128)(2,1)S(1)}, bf16[128,512]{1,0:T(8,128)(2,1)S(1)}, u32[]{:S(2)}, u32[]{:S(2)}) %collective-permute-start.24) | collective-permute-done | bytes 131104 | tf_op jit(solution)/shard_map/ppermute | solution.py:308
  93.3 1.0 %collective-permute-done.25.refs_5_ = bf16[128,512]{1,0:T(8,128)(2,1)S(1)} collective-permute-done((bf16[128,512]{1,0:T(8,128)(2,1)S(1)}, bf16[128,512]{1,0:T(8,128)(2,1)S(1)}, u32[]{:S(2)}, u32[]{:S(2)}) %collective-permute-start.25) | collective-permute-done | bytes 131104 | tf_op jit(solution)/shard_map/ppermute | solution.py:308
  94.3 2.5 %collective-permute-done.27.refs_7_ = bf16[128,512]{1,0:T(8,128)(2,1)S(1)} collective-permute-done((bf16[128,512]{1,0:T(8,128)(2,1)S(1)}, bf16[128,512]{1,0:T(8,128)(2,1)S(1)}, u32[]{:S(2)}, u32[]{:S(2)}) %collective-permute-start.27) | collective-permute-done | bytes 131104 | tf_op jit(solution)/shard_map/ppermute | solution.py:308
  96.8 0.8 finish.1
  (29 shorter events, 0.2 us)
Async XLA Ops:
  0.0 35.6 %copy-start.2 = (bf16[1,32,4096]{2,1,0:T(8,128)(2,1)S(1)}, bf16[1,32,4096]{2,1,0:T(8,128)(2,1)}, u32[]{:S(2)}) copy-start(bf16[1,32,4096]{2,1,0:T(8,128)(2,1)} %param.6) | copy-start | bytes 786436
  0.0 18.3 %collective-permute-start.4 = (bf16[512,4096]{1,0:T(8,128)(2,1)}, bf16[512,4096]{1,0:T(8,128)(2,1)S(1)}, u32[]{:S(2)}, u32[]{:S(2)}) collective-permute-start(bf16[512,4096]{1,0:T(8,128)(2,1)} %bitcast.37), channel_id=1, source_target_pairs={{0,8},{8,0},{16,24},{24,16},{32,40},{40,32},{48,56},{56,48},{64,72... | collective-permute-start | bytes 12582920 | tf_op jit(solution)/shard_map/ppermute | solution.py:40
  0.0 29.3 %collective-permute-start.8 = (bf16[32,4096]{1,0:T(8,128)(2,1)}, bf16[32,4096]{1,0:T(8,128)(2,1)S(1)}, u32[]{:S(2)}, u32[]{:S(2)}) collective-permute-start(bf16[32,4096]{1,0:T(8,128)(2,1)} %bitcast.31), channel_id=1, source_target_pairs={{0,16},{8,24},{16,32},{24,40},{32,48},{40,56},{48,0},{56,8},{64,80... | collective-permute-start | bytes 786440 | tf_op jit(solution)/shard_map/ppermute | solution.py:40
  3.4 26.0 %collective-permute-start.9 = (bf16[32,4096]{1,0:T(8,128)(2,1)}, bf16[32,4096]{1,0:T(8,128)(2,1)S(1)}, u32[]{:S(2)}, u32[]{:S(2)}) collective-permute-start(bf16[32,4096]{1,0:T(8,128)(2,1)} %bitcast.32), channel_id=1, source_target_pairs={{0,48},{8,56},{16,0},{24,8},{32,16},{40,24},{48,32},{56,40},{64,11... | collective-permute-start | bytes 786440 | tf_op jit(solution)/shard_map/ppermute | solution.py:40
  6.5 0.7 copy-start.3
  7.2 0.7 copy-start.4
  7.8 0.7 copy-start.5
  8.5 1.3 %collective-permute-start = (f32[8,128]{1,0:T(8,128)S(1)}, f32[8,128]{1,0:T(8,128)S(1)}, u32[]{:S(2)}, u32[]{:S(2)}) collective-permute-start(f32[8,128]{1,0:T(8,128)S(1)} %pack.1.refs_0_), channel_id=1, source_target_pairs={{0,8},{8,0},{16,24},{24,16},{32,40},{40,32},{48,56},{56,48},{64,72... | collective-permute-start | bytes 12296 | tf_op jit(solution)/shard_map/ppermute | solution.py:40
  9.8 3.7 %collective-permute-start.1 = (f32[16,128]{1,0:T(8,128)S(1)}, f32[16,128]{1,0:T(8,128)S(1)}, u32[]{:S(2)}, u32[]{:S(2)}) collective-permute-start(f32[16,128]{1,0:T(8,128)S(1)} %join.7.refs_0_), channel_id=1, source_target_pairs={{0,64},{8,72},{16,80},{24,88},{32,96},{40,104},{48,112},{56,120},{... | collective-permute-start | bytes 24584 | tf_op jit(solution)/shard_map/ppermute | solution.py:40
  10.0 5.2 %collective-permute-start.2 = (f32[16,128]{1,0:T(8,128)S(1)}, f32[16,128]{1,0:T(8,128)S(1)}, u32[]{:S(2)}, u32[]{:S(2)}) collective-permute-start(f32[16,128]{1,0:T(8,128)S(1)} %join.7.refs_0_), channel_id=1, source_target_pairs={{0,128},{8,136},{16,144},{24,152},{32,160},{40,168},{48,176},{56,1... | collective-permute-start | bytes 24584 | tf_op jit(solution)/shard_map/ppermute | solution.py:40
  13.4 4.9 %collective-permute-start.3 = (f32[16,128]{1,0:T(8,128)S(1)}, f32[16,128]{1,0:T(8,128)S(1)}, u32[]{:S(2)}, u32[]{:S(2)}) collective-permute-start(f32[16,128]{1,0:T(8,128)S(1)} %join.7.refs_0_), channel_id=1, source_target_pairs={{0,192},{8,200},{16,208},{24,216},{32,224},{40,232},{48,240},{56,2... | collective-permute-start | bytes 24584 | tf_op jit(solution)/shard_map/ppermute | solution.py:40
  18.3 2.0 %copy-start = (bf16[512,4096]{1,0:T(8,128)(2,1)}, bf16[512,4096]{1,0:T(8,128)(2,1)S(1)}, u32[]{:S(2)}) copy-start(bf16[512,4096]{1,0:T(8,128)(2,1)S(1)} %collective-permute-done.4.refs_4_.x_ref) | copy-start | bytes 12582916
  20.3 9.1 %collective-permute-start.5 = (f32[64,128]{1,0:T(8,128)S(1)}, f32[64,128]{1,0:T(8,128)S(1)}, u32[]{:S(2)}, u32[]{:S(2)}) collective-permute-start(f32[64,128]{1,0:T(8,128)S(1)} %join.8.refs_0_), channel_id=1, source_target_pairs={{0,16},{8,24},{16,32},{24,40},{32,48},{40,56},{48,0},{56,8},{64,80... | collective-permute-start | bytes 98312 | tf_op jit(solution)/shard_map/ppermute | solution.py:40
  21.6 7.8 %collective-permute-start.6 = (f32[64,128]{1,0:T(8,128)S(1)}, f32[64,128]{1,0:T(8,128)S(1)}, u32[]{:S(2)}, u32[]{:S(2)}) collective-permute-start(f32[64,128]{1,0:T(8,128)S(1)} %join.8.refs_0_), channel_id=1, source_target_pairs={{0,32},{8,40},{16,48},{24,56},{32,0},{40,8},{48,16},{56,24},{64,96... | collective-permute-start | bytes 98312 | tf_op jit(solution)/shard_map/ppermute | solution.py:40
  26.3 8.1 %collective-permute-start.7 = (f32[64,128]{1,0:T(8,128)S(1)}, f32[64,128]{1,0:T(8,128)S(1)}, u32[]{:S(2)}, u32[]{:S(2)}) collective-permute-start(f32[64,128]{1,0:T(8,128)S(1)} %join.8.refs_0_), channel_id=1, source_target_pairs={{0,48},{8,56},{16,0},{24,8},{32,16},{40,24},{48,32},{56,40},{64,11... | collective-permute-start | bytes 98312 | tf_op jit(solution)/shard_map/ppermute | solution.py:40
  29.5 10.9 %collective-permute-start.10 = (bf16[16,4096]{1,0:T(8,128)(2,1)S(1)}, bf16[16,4096]{1,0:T(8,128)(2,1)S(1)}, u32[]{:S(2)}, u32[]{:S(2)}) collective-permute-start(bf16[16,4096]{1,0:T(8,128)(2,1)S(1)} %get-tuple-element.17.refs_3_), channel_id=1, source_target_pairs={{0,16},{8,24},{16,32},{24,40},{32,48},{40,56},{48,0},{56,8},{64,80... | collective-permute-start | bytes 393224 | tf_op jit(solution)/shard_map/ppermute | solution.py:40
  33.7 6.9 %collective-permute-start.11 = (bf16[16,4096]{1,0:T(8,128)(2,1)S(1)}, bf16[16,4096]{1,0:T(8,128)(2,1)S(1)}, u32[]{:S(2)}, u32[]{:S(2)}) collective-permute-start(bf16[16,4096]{1,0:T(8,128)(2,1)S(1)} %get-tuple-element.18), channel_id=1, source_target_pairs={{0,48},{8,56},{16,0},{24,8},{32,16},{40,24},{48,32},{56,40},{64,11... | collective-permute-start | bytes 393224 | tf_op jit(solution)/shard_map/ppermute | solution.py:40
  38.2 5.8 %copy-start.1 = (bf16[512,4096]{1,0:T(8,128)(2,1)S(1)}, bf16[512,4096]{1,0:T(8,128)(2,1)}, u32[]{:S(2)}) copy-start(bf16[512,4096]{1,0:T(8,128)(2,1)} %copy-done) | copy-start | bytes 12582916
  38.2 23.3 %collective-permute-start.13 = (bf16[96,4096]{1,0:T(8,128)(2,1)S(1)}, bf16[96,4096]{1,0:T(8,128)(2,1)S(1)}, u32[]{:S(2)}, u32[]{:S(2)}) collective-permute-start(bf16[96,4096]{1,0:T(8,128)(2,1)S(1)} %rotate.2.refs_2_.refs_0_), channel_id=1, source_target_pairs={{0,64},{8,72},{16,80},{24,88},{32,96},{40,104},{48,112},{56,120},{... | collective-permute-start | bytes 2359304 | tf_op jit(solution)/shard_map/ppermute | solution.py:40
  38.5 23.4 %collective-permute-start.14 = (bf16[96,4096]{1,0:T(8,128)(2,1)S(1)}, bf16[96,4096]{1,0:T(8,128)(2,1)S(1)}, u32[]{:S(2)}, u32[]{:S(2)}) collective-permute-start(bf16[96,4096]{1,0:T(8,128)(2,1)S(1)} %rotate.2.refs_2_.refs_0_), channel_id=1, source_target_pairs={{0,192},{8,200},{16,208},{24,216},{32,224},{40,232},{48,240},{56,2... | collective-permute-start | bytes 2359304 | tf_op jit(solution)/shard_map/ppermute | solution.py:40
  42.0 19.6 %collective-permute-start.15 = (bf16[32,4096]{1,0:T(8,128)(2,1)S(1)}, bf16[32,4096]{1,0:T(8,128)(2,1)S(1)}, u32[]{:S(2)}, u32[]{:S(2)}) collective-permute-start(bf16[32,4096]{1,0:T(8,128)(2,1)S(1)} %rotate.3.refs_0_.refs_1_), channel_id=1, source_target_pairs={{0,64},{8,72},{16,80},{24,88},{32,96},{40,104},{48,112},{56,120},{... | collective-permute-start | bytes 786440 | tf_op jit(solution)/shard_map/ppermute | solution.py:40
  43.3 20.5 %collective-permute-start.16 = (bf16[32,4096]{1,0:T(8,128)(2,1)S(1)}, bf16[32,4096]{1,0:T(8,128)(2,1)S(1)}, u32[]{:S(2)}, u32[]{:S(2)}) collective-permute-start(bf16[32,4096]{1,0:T(8,128)(2,1)S(1)} %rotate.3.refs_0_.refs_1_), channel_id=1, source_target_pairs={{0,192},{8,200},{16,208},{24,216},{32,224},{40,232},{48,240},{56,2... | collective-permute-start | bytes 786440 | tf_op jit(solution)/shard_map/ppermute | solution.py:40
  44.4 2.2 %copy-start.6 = (bf16[1,512,4096]{2,1,0:T(8,128)(2,1)S(1)}, bf16[1,512,4096]{2,1,0:T(8,128)(2,1)}, u32[]{:S(2)}) copy-start(bf16[1,512,4096]{2,1,0:T(8,128)(2,1)} %param.7) | copy-start | bytes 12582916
  46.0 30.5 %collective-permute-start.12 = (bf16[128,512]{1,0:T(8,128)(2,1)S(1)}, bf16[128,512]{1,0:T(8,128)(2,1)S(1)}, u32[]{:S(2)}, u32[]{:S(2)}) collective-permute-start(bf16[128,512]{1,0:T(8,128)(2,1)S(1)} %convolution_convert_fusion.4), channel_id=1, source_target_pairs={{0,8},{8,0},{16,24},{24,16},{32,40},{40,32},{48,56},{56,48},{64,72... | collective-permute-start | bytes 393224 | tf_op jit(solution)/shard_map/ppermute | solution.py:40
  61.6 10.0 %collective-permute-start.18 = (bf16[64,4096]{1,0:T(8,128)(2,1)S(1)}, bf16[64,4096]{1,0:T(8,128)(2,1)S(1)}, u32[]{:S(2)}, u32[]{:S(2)}) collective-permute-start(bf16[64,4096]{1,0:T(8,128)(2,1)S(1)} %join.10.refs_4_), channel_id=1, source_target_pairs={{0,64},{8,72},{16,80},{24,88},{32,96},{40,104},{48,112},{56,120},{... | collective-permute-start | bytes 1572872 | tf_op jit(solution)/shard_map/ppermute | solution.py:40
  62.0 11.1 %collective-permute-start.19 = (bf16[64,4096]{1,0:T(8,128)(2,1)S(1)}, bf16[64,4096]{1,0:T(8,128)(2,1)S(1)}, u32[]{:S(2)}, u32[]{:S(2)}) collective-permute-start(bf16[64,4096]{1,0:T(8,128)(2,1)S(1)} %join.11.refs_5_), channel_id=1, source_target_pairs={{0,192},{8,200},{16,208},{24,216},{32,224},{40,232},{48,240},{56,2... | collective-permute-start | bytes 1572872 | tf_op jit(solution)/shard_map/ppermute | solution.py:40
  65.2 11.4 %collective-permute-start.17 = (bf16[256,512]{1,0:T(8,128)(2,1)S(1)}, bf16[256,512]{1,0:T(8,128)(2,1)S(1)}, u32[]{:S(2)}, u32[]{:S(2)}) collective-permute-start(bf16[256,512]{1,0:T(8,128)(2,1)S(1)} %convolution_convert_fusion), channel_id=1, source_target_pairs={{0,8},{8,0},{16,24},{24,16},{32,40},{40,32},{48,56},{56,48},{64,72... | collective-permute-start | bytes 786440 | tf_op jit(solution)/shard_map/ppermute | solution.py:40
  74.7 1.9 %collective-permute-start.20 = (bf16[128,512]{1,0:T(8,128)(2,1)S(1)}, bf16[128,512]{1,0:T(8,128)(2,1)S(1)}, u32[]{:S(2)}, u32[]{:S(2)}) collective-permute-start(bf16[128,512]{1,0:T(8,128)(2,1)S(1)} %convolution_convert_fusion.2), channel_id=1, source_target_pairs={{0,8},{8,0},{16,24},{24,16},{32,40},{40,32},{48,56},{56,48},{64,72... | collective-permute-start | bytes 393224 | tf_op jit(solution)/shard_map/ppermute | solution.py:40
  77.4 9.2 %collective-permute-start.21 = (bf16[128,512]{1,0:T(8,128)(2,1)S(1)}, bf16[128,512]{1,0:T(8,128)(2,1)S(1)}, u32[]{:S(2)}, u32[]{:S(2)}) collective-permute-start(bf16[128,512]{1,0:T(8,128)(2,1)S(1)} %bitcast.44), channel_id=1, source_target_pairs={{0,6},{1,7},{2,4},{3,5},{4,2},{5,3},{6,0},{7,1},{8,14},{9,15},{10,... | collective-permute-start | bytes 393224 | tf_op jit(solution)/shard_map/ppermute | solution.py:308
  81.2 10.6 %collective-permute-start.22 = (bf16[128,512]{1,0:T(8,128)(2,1)S(1)}, bf16[128,512]{1,0:T(8,128)(2,1)S(1)}, u32[]{:S(2)}, u32[]{:S(2)}) collective-permute-start(bf16[128,512]{1,0:T(8,128)(2,1)S(1)} %bitcast.43), channel_id=1, source_target_pairs={{0,2},{1,3},{2,0},{3,1},{4,6},{5,7},{6,4},{7,5},{8,10},{9,11},{10,... | collective-permute-start | bytes 393224 | tf_op jit(solution)/shard_map/ppermute | solution.py:308
  81.7 10.1 %collective-permute-start.23 = (bf16[128,512]{1,0:T(8,128)(2,1)S(1)}, bf16[128,512]{1,0:T(8,128)(2,1)S(1)}, u32[]{:S(2)}, u32[]{:S(2)}) collective-permute-start(bf16[128,512]{1,0:T(8,128)(2,1)S(1)} %bitcast.42), channel_id=1, source_target_pairs={{0,5},{1,6},{2,7},{3,4},{4,1},{5,2},{6,3},{7,0},{8,13},{9,14},{10,... | collective-permute-start | bytes 393224 | tf_op jit(solution)/shard_map/ppermute | solution.py:308
  83.4 9.9 %collective-permute-start.24 = (bf16[128,512]{1,0:T(8,128)(2,1)S(1)}, bf16[128,512]{1,0:T(8,128)(2,1)S(1)}, u32[]{:S(2)}, u32[]{:S(2)}) collective-permute-start(bf16[128,512]{1,0:T(8,128)(2,1)S(1)} %bitcast.41), channel_id=1, source_target_pairs={{0,7},{1,4},{2,5},{3,6},{4,3},{5,0},{6,1},{7,2},{8,15},{9,12},{10,... | collective-permute-start | bytes 393224 | tf_op jit(solution)/shard_map/ppermute | solution.py:308
  85.8 8.5 %collective-permute-start.25 = (bf16[128,512]{1,0:T(8,128)(2,1)S(1)}, bf16[128,512]{1,0:T(8,128)(2,1)S(1)}, u32[]{:S(2)}, u32[]{:S(2)}) collective-permute-start(bf16[128,512]{1,0:T(8,128)(2,1)S(1)} %bitcast.40), channel_id=1, source_target_pairs={{0,4},{1,5},{2,6},{3,7},{4,0},{5,1},{6,2},{7,3},{8,12},{9,13},{10,... | collective-permute-start | bytes 393224 | tf_op jit(solution)/shard_map/ppermute | solution.py:308
  86.6 7.7 %collective-permute-start.26 = (bf16[128,512]{1,0:T(8,128)(2,1)S(1)}, bf16[128,512]{1,0:T(8,128)(2,1)S(1)}, u32[]{:S(2)}, u32[]{:S(2)}) collective-permute-start(bf16[128,512]{1,0:T(8,128)(2,1)S(1)} %bitcast.39), channel_id=1, source_target_pairs={{0,1},{1,2},{2,3},{3,0},{4,5},{5,6},{6,7},{7,4},{8,9},{9,10},{10,1... | collective-permute-start | bytes 393224 | tf_op jit(solution)/shard_map/ppermute | solution.py:308
  91.8 5.0 %collective-permute-start.27 = (bf16[128,512]{1,0:T(8,128)(2,1)S(1)}, bf16[128,512]{1,0:T(8,128)(2,1)S(1)}, u32[]{:S(2)}, u32[]{:S(2)}) collective-permute-start(bf16[128,512]{1,0:T(8,128)(2,1)S(1)} %bitcast.38), channel_id=1, source_target_pairs={{0,3},{1,0},{2,1},{3,2},{4,7},{5,4},{6,5},{7,6},{8,11},{9,8},{10,9... | collective-permute-start | bytes 393224 | tf_op jit(solution)/shard_map/ppermute | solution.py:308
where the time goes:
time: 98.1 us; the launch traced here: 97.6 us
  starting transfers between devices  40.3 us (41%)
  waiting for transfers between devices  35.6 us (36%)
  matrix products  8.8 us (9%)
  Pallas kernels  7.38 us (8%)
  local copies, waits for them, and re-layouts  4.53 us (5%)
    ppermute x21, starting transfers between devices, send(): return lax.ppermute(x, 'example', example_shift(dy, dz, dc))  30.3 us
    ppermute x21, waiting for transfers between devices, send(): return lax.ppermute(x, 'example', example_shift(dy, dz, dc))  26.2 us
    ppermute x7, starting transfers between devices, spread_over_layers(): lax.ppermute(ready[dl * NX + dx], 'layer', layer_shift(dl, dx))  9.97 us
    ppermute x7, waiting for transfers between devices, spread_over_layers(): lax.ppermute(ready[dl * NX + dx], 'layer', layer_shift(dl, dx))  9.42 us
    dot_general x6, matrix products, scores_of(): lax.dot_general(conditioned, documents, (((1,), (1,)), ((), ())), preferr...  8.8 us
    unnamed x14, local copies, waits for them, and re-layouts  4.46 us
    pallas_call x2, Pallas kernels, rotate(): pl.pallas_call(functools.partial(rotate_kernel, CHUNK, len(blocks)), out_...  3.98 us
  transfers between devices with their start and end apart: 28, of which 13 were waited for; matrix products, arithmetic and copies ran while one was open for 9% of the time, Pallas kernels for 6%

commit v1 on v0

--- a/solution.py
+++ b/solution.py
@@ -304,7 +304,7 @@
 def spread_over_layers(ready):
     ready = ready.reshape(NL * NX, 4 * ROWS, ready.shape[-1])
     parts = [ready[0]]
-    for dl, dx in ((1, 2), (0, 2), (1, 1), (1, 3), (1, 0), (0, 1), (0, 3)):
+    for dl, dx in ((1, 0), (0, 1), (1, 2), (0, 2), (1, 1), (1, 3), (0, 3)):
         parts.append(lax.ppermute(ready[dl * NX + dx], "layer", layer_shift(dl, dx)))
     return parts
 
@@ -342,7 +342,7 @@
     row = pack(in_basis[0], eigenvalues[0], out_basis[0])
     pair = join([row, send(row, dc=1)], [])
     column = [send(pair, dy=d) for d in range(1, NY)]
-    plane = join([pair] + column, [docs_there])
+    plane = join([pair] + column, near)
     pieces = [plane] + [send(plane, dz=d) for d in range(1, NZ)]
     tables = prepare(place, damping, pieces, [])
 
@@ -354,22 +354,26 @@
     other = rotate(tables, far, [side], 20_000_000_000)
     other_y = both_ways(other, "dy")
 
-    low = join([side_y[1]], [], [(ROWS, 3 * ROWS)])
-    high = join([side_y[0], other_y[0]], [], [(0, ROWS), (0, ROWS)])
+    docs_other = held(docs_there, [other])
+
+    def scored(blocks, after):
+        conditioned = join(blocks, after)
+        theirs = send(scores_of(conditioned, docs_other), dc=1)
+        return [scores_of(conditioned, docs), theirs]
+
+    parts = scored((side, other), [docs_other])
+
+    low = join([side_y[1]], parts[:1], [(ROWS, 3 * ROWS)])
+    high = join([side_y[0], other_y[0]], parts[:1], [(0, ROWS), (0, ROWS)])
     side_far = send(high, dy=1), send(low, dy=-1)
-
-    docs_other = held(docs_there, [other])
+    parts += scored((*side_y, *other_y), [high, low])
+    parts += scored(side_far, parts[2:3])
 
     offsets = [
         [(0, 0), (0, 1), (0, -1), (0, 2)],
         [(1, 0), (1, 1), (1, -1), (-1, 0), (-1, 1), (-1, -1), (1, 2), (-1, 2)],
         [(2, 0), (2, 2), (2, 1), (2, -1)],
     ]
-    parts = []
-    for blocks, after in (((side, other), [docs_other]), ((*side_y, *other_y), [high, low]), (side_far, [])):
-        conditioned = join(blocks, after + parts[-2:-1])
-        theirs = send(scores_of(conditioned, docs_other), dc=1)
-        parts += [scores_of(conditioned, docs), theirs]
     return finish(spread_over_layers(arrange(place, offsets, parts, [])))
 
 

time: 98.1 us -> 102 us (1.040)
  waiting for transfers between devices: 35.6 us -> 38.5 us
  Pallas kernels: 7.38 us -> 9.28 us
  local copies, waits for them, and re-layouts: 4.53 us -> 3.5 us
    ppermute x21, waiting for transfers between devices: 26.2 us -> 31.6 us  [send(): return lax.ppermute(x, 'example', example_shift(dy, dz, dc))]
    ppermute x7, waiting for transfers between devices: 9.42 us -> 6.9 us  [spread_over_layers(): lax.ppermute(ready[dl * NX + dx], 'layer', layer_shift(dl, dx))]
    pallas_call x1, Pallas kernels: 0.28 us -> 2.19 us  [held(): pl.pallas_call(held_kernel, out_shape=jax.ShapeDtypeStruct(x.shape, x.dty...]
    ppermute x21, starting transfers between devices: 30.3 us -> 29 us  [send(): return lax.ppermute(x, 'example', example_shift(dy, dz, dc))]
    ppermute x7, starting transfers between devices: 9.97 us -> 11.2 us  [spread_over_layers(): lax.ppermute(ready[dl * NX + dx], 'layer', layer_shift(dl, dx))]
    unnamed x14 -> x10, local copies, waits for them, and re-layouts: 4.46 us -> 3.43 us
  transfers between devices with their start and end apart: 28 -> 28, of which waited for: 13 -> 12; matrix products, arithmetic and copies ran while one was open for 9% -> 9% of each run, Pallas kernels for 6% -> 8%
where the time goes in v1:
time: 102 us; the launch traced here: 101 us
  starting transfers between devices  40.3 us (40%)
  waiting for transfers between devices  38.5 us (38%)
  Pallas kernels  9.28 us (9%)
  matrix products  8.78 us (9%)
  local copies, waits for them, and re-layouts  3.5 us (3%)
    ppermute x21, waiting for transfers between devices, send(): return lax.ppermute(x, 'example', example_shift(dy, dz, dc))  31.6 us
    ppermute x21, starting transfers between devices, send(): return lax.ppermute(x, 'example', example_shift(dy, dz, dc))  29 us
    ppermute x7, starting transfers between devices, spread_over_layers(): lax.ppermute(ready[dl * NX + dx], 'layer', layer_shift(dl, dx))  11.2 us
    dot_general x6, matrix products, scores_of(): lax.dot_general(conditioned, documents, (((1,), (1,)), ((), ())), preferr...  8.78 us
    ppermute x7, waiting for transfers between devices, spread_over_layers(): lax.ppermute(ready[dl * NX + dx], 'layer', layer_shift(dl, dx))  6.9 us
    pallas_call x2, Pallas kernels, rotate(): pl.pallas_call(functools.partial(rotate_kernel, CHUNK, len(blocks)), out_...  3.98 us
    unnamed x10, local copies, waits for them, and re-layouts  3.43 us
    pallas_call x1, Pallas kernels, held(): pl.pallas_call(held_kernel, out_shape=jax.ShapeDtypeStruct(x.shape, x.dty...  2.19 us
  transfers between devices with their start and end apart: 28, of which 12 were waited for; matrix products, arithmetic and copies ran while one was open for 9% of the time, Pallas kernels for 8%

profile of v1, /device:TPU:24, one launch (start us, length us, event | category | flops | bytes accessed | tf_op | source)
XLA Modules:
  0.0 101.3 jit_solution(8508018753258678353)
XLA Ops:
  0.0 0.0 collective-permute-start.11
  0.0 3.3 %collective-permute-start.4 = (bf16[32,4096]{1,0:T(8,128)(2,1)}, bf16[32,4096]{1,0:T(8,128)(2,1)S(1)}, u32[]{:S(2)}, u32[]{:S(2)}) collective-permute-start(bf16[32,4096]{1,0:T(8,128)(2,1)} %bitcast.31), channel_id=1, source_target_pairs={{0,16},{8,24},{16,32},{24,40},{32,48},{40,56},{48,0},{56,8},{64,80... | collective-permute-start | bytes 786440 | tf_op jit(solution)/shard_map/ppermute | solution.py:40
  3.3 3.1 %collective-permute-start.5 = (bf16[32,4096]{1,0:T(8,128)(2,1)}, bf16[32,4096]{1,0:T(8,128)(2,1)S(1)}, u32[]{:S(2)}, u32[]{:S(2)}) collective-permute-start(bf16[32,4096]{1,0:T(8,128)(2,1)} %bitcast.32), channel_id=1, source_target_pairs={{0,48},{8,56},{16,0},{24,8},{32,16},{40,24},{48,32},{56,40},{64,11... | collective-permute-start | bytes 786440 | tf_op jit(solution)/shard_map/ppermute | solution.py:40
  6.4 0.7 copy-done.1
  7.1 0.7 copy-done.2
  7.7 0.7 copy-done.3
  8.4 0.2 collective-permute-start
  8.7 1.0 collective-permute-done.refs_1_
  9.7 0.2 collective-permute-start.1
  9.9 2.6 %collective-permute-start.2 = (f32[16,128]{1,0:T(8,128)S(1)}, f32[16,128]{1,0:T(8,128)S(1)}, u32[]{:S(2)}, u32[]{:S(2)}) collective-permute-start(f32[16,128]{1,0:T(8,128)S(1)} %join.7.refs_0_), channel_id=1, source_target_pairs={{0,128},{8,136},{16,144},{24,152},{32,160},{40,168},{48,176},{56,1... | collective-permute-start | bytes 24584 | tf_op jit(solution)/shard_map/ppermute | solution.py:40
  12.5 0.8 collective-permute-done.1.refs_1_
  13.3 0.7 collective-permute-start.3
  14.1 1.0 collective-permute-done.2.refs_2_
  15.1 3.1 %collective-permute-done.3.refs_3_ = f32[16,128]{1,0:T(8,128)S(1)} collective-permute-done((f32[16,128]{1,0:T(8,128)S(1)}, f32[16,128]{1,0:T(8,128)S(1)}, u32[]{:S(2)}, u32[]{:S(2)}) %collective-permute-start.3) | collective-permute-done | bytes 8224 | tf_op jit(solution)/shard_map/ppermute | solution.py:40
  18.2 2.1 %collective-permute-done.5.refs_5_.ahead_ref.refs_2_ = bf16[32,4096]{1,0:T(8,128)(2,1)S(1)} collective-permute-done((bf16[32,4096]{1,0:T(8,128)(2,1)}, bf16[32,4096]{1,0:T(8,128)(2,1)S(1)}, u32[]{:S(2)}, u32[]{:S(2)}) %collective-permute-start.5) | collective-permute-done | bytes 262176 | tf_op jit(solution)/shard_map/ppermute | solution.py:40
  20.3 3.7 %collective-permute-start.6 = (f32[64,128]{1,0:T(8,128)S(1)}, f32[64,128]{1,0:T(8,128)S(1)}, u32[]{:S(2)}, u32[]{:S(2)}) collective-permute-start(f32[64,128]{1,0:T(8,128)S(1)} %join.8.refs_0_), channel_id=1, source_target_pairs={{0,16},{8,24},{16,32},{24,40},{32,48},{40,56},{48,0},{56,8},{64,80... | collective-permute-start | bytes 98312 | tf_op jit(solution)/shard_map/ppermute | solution.py:40
  24.1 1.3 %collective-permute-start.7 = (f32[64,128]{1,0:T(8,128)S(1)}, f32[64,128]{1,0:T(8,128)S(1)}, u32[]{:S(2)}, u32[]{:S(2)}) collective-permute-start(f32[64,128]{1,0:T(8,128)S(1)} %join.8.refs_0_), channel_id=1, source_target_pairs={{0,32},{8,40},{16,48},{24,56},{32,0},{40,8},{48,16},{56,24},{64,96... | collective-permute-start | bytes 98312 | tf_op jit(solution)/shard_map/ppermute | solution.py:40
  25.3 2.7 %collective-permute-start.8 = (f32[64,128]{1,0:T(8,128)S(1)}, f32[64,128]{1,0:T(8,128)S(1)}, u32[]{:S(2)}, u32[]{:S(2)}) collective-permute-start(f32[64,128]{1,0:T(8,128)S(1)} %join.8.refs_0_), channel_id=1, source_target_pairs={{0,48},{8,56},{16,0},{24,8},{32,16},{40,24},{48,32},{56,40},{64,11... | collective-permute-start | bytes 98312 | tf_op jit(solution)/shard_map/ppermute | solution.py:40
  28.1 4.1 %collective-permute-done.7.refs_2_.refs_1_ = f32[64,128]{1,0:T(8,128)S(1)} collective-permute-done((f32[64,128]{1,0:T(8,128)S(1)}, f32[64,128]{1,0:T(8,128)S(1)}, u32[]{:S(2)}, u32[]{:S(2)}) %collective-permute-start.7) | collective-permute-done | bytes 32800 | tf_op jit(solution)/shard_map/ppermute | solution.py:40
  32.2 0.3 collective-permute-start.9
  32.5 3.9 %collective-permute-start.10 = (bf16[16,4096]{1,0:T(8,128)(2,1)S(1)}, bf16[16,4096]{1,0:T(8,128)(2,1)S(1)}, u32[]{:S(2)}, u32[]{:S(2)}) collective-permute-start(bf16[16,4096]{1,0:T(8,128)(2,1)S(1)} %get-tuple-element.18), channel_id=1, source_target_pairs={{0,48},{8,56},{16,0},{24,8},{32,16},{40,24},{48,32},{56,40},{64,11... | collective-permute-start | bytes 393224 | tf_op jit(solution)/shard_map/ppermute | solution.py:40
  36.4 0.1 pad_add_fusion.place_ref
  37.1 1.2 %prepare.1 = (bf16[512,256]{1,0:T(8,128)(2,1)S(1)}, bf16[512,256]{1,0:T(8,128)(2,1)S(1)}, bf16[256,128]{1,0:T(8,128)(2,1)S(1)}, bf16[256,256]{1,0:T(8,128)(2,1)S(1)}, f32[256,128]{1,0:T(8,128)S(1)}) custom-call(s32[2]{0:T(128)S(1)} %pad_add_fusion.place_ref, f32[1]{0:T(128)S(6)} %copy.7.damp_ref, f32[64,128]{1,0:T(8,128)S(1)} %join.8.refs_0_, ...), custom_call_target="tpu_custom_call" | custom-call | flops 200000000 | bytes 1048576 | tf_op jit(solution)/shard_map/prepare/pallas_call | solution.py:171
  38.3 0.0 copy-start
  38.4 0.9 copy-done
  39.3 2.6 %rotate.2.refs_2_.refs_0_ = bf16[96,4096]{1,0:T(8,128)(2,1)S(1)} custom-call(bf16[512,256]{1,0:T(8,128)(2,1)S(1)} %get-tuple-element.12.left_ref, bf16[512,256]{1,0:T(8,128)(2,1)S(1)} %get-tuple-element.13.right_ref, bf16[256,128]{1,0:T(8,128)(2,1)S(1)} %get-tuple-element.14.in_ref, bf16[256,256]{1,0:T(8,128)(2,1)S(1)} %get-tuple-element.15.back_ref, ...), custom_call_target="tpu_custom_call" | custom-call | tf_op jit(solution)/shard_map/rotate/pallas_call | solution.py:240
  41.9 0.3 collective-permute-start.13
  42.2 1.8 %collective-permute-start.14 = (bf16[96,4096]{1,0:T(8,128)(2,1)S(1)}, bf16[96,4096]{1,0:T(8,128)(2,1)S(1)}, u32[]{:S(2)}, u32[]{:S(2)}) collective-permute-start(bf16[96,4096]{1,0:T(8,128)(2,1)S(1)} %rotate.2.refs_2_.refs_0_), channel_id=1, source_target_pairs={{0,192},{8,200},{16,208},{24,216},{32,224},{40,232},{48,240},{56,2... | collective-permute-start | bytes 2359304 | tf_op jit(solution)/shard_map/ppermute | solution.py:40
  44.0 1.4 %rotate.3.refs_0_.refs_1_ = bf16[32,4096]{1,0:T(8,128)(2,1)S(1)} custom-call(bf16[512,256]{1,0:T(8,128)(2,1)S(1)} %get-tuple-element.12.left_ref, bf16[512,256]{1,0:T(8,128)(2,1)S(1)} %get-tuple-element.13.right_ref, bf16[256,128]{1,0:T(8,128)(2,1)S(1)} %get-tuple-element.14.in_ref, bf16[256,256]{1,0:T(8,128)(2,1)S(1)} %get-tuple-element.15.back_ref, ...), custom_call_target="tpu_custom_call" | custom-call | flops 20000000000 | tf_op jit(solution)/shard_map/rotate/pallas_call | solution.py:240
  45.4 1.6 %collective-permute-start.15 = (bf16[32,4096]{1,0:T(8,128)(2,1)S(1)}, bf16[32,4096]{1,0:T(8,128)(2,1)S(1)}, u32[]{:S(2)}, u32[]{:S(2)}) collective-permute-start(bf16[32,4096]{1,0:T(8,128)(2,1)S(1)} %rotate.3.refs_0_.refs_1_), channel_id=1, source_target_pairs={{0,64},{8,72},{16,80},{24,88},{32,96},{40,104},{48,112},{56,120},{... | collective-permute-start | bytes 786440 | tf_op jit(solution)/shard_map/ppermute | solution.py:40
  47.0 0.5 collective-permute-start.16
  47.5 2.2 %held.1.refs_2_ = bf16[512,4096]{1,0:T(8,128)(2,1)S(1)} custom-call(bf16[512,4096]{1,0:T(8,128)(2,1)} %collective-permute-done.11.x_ref, bf16[32,4096]{1,0:T(8,128)(2,1)S(1)} %rotate.3.refs_0_.refs_1_), custom_call_target="tpu_custom_call" | custom-call | bytes 8388608 | tf_op jit(solution)/shard_map/held/pallas_call | solution.py:61
  49.7 0.1 join.9
  49.8 0.0 copy-start.4
  49.8 1.6 %convolution_convert_fusion.4 = bf16[128,512]{1,0:T(8,128)(2,1)S(1)} fusion(bf16[128,4096]{1,0:T(8,128)(2,1)S(1)} %join.9, bf16[512,4096]{1,0:T(8,128)(2,1)S(1)} %held.1.refs_2_), kind=kOutput, calls=%fused_computation.4 | convolution fusion | flops 536936448 | bytes 5373952 | tf_op jit(solution)/shard_map/dot_general | solution.py:252
  51.4 0.1 collective-permute-start.12
  51.5 0.5 copy-done.4
  52.0 1.5 %convolution_convert_fusion.5.refs_2_.refs_1_.refs_0_ = bf16[128,512]{1,0:T(8,128)(2,1)S(1)} fusion(bf16[128,4096]{1,0:T(8,128)(2,1)S(1)} %join.9, bf16[1,512,4096]{2,1,0:T(8,128)(2,1)S(1)} %copy-done.4), kind=kOutput, calls=%fused_computation.5 | convolution fusion | flops 536936448 | bytes 5373952 | tf_op jit(solution)/shard_map/dot_general | solution.py:252
  53.5 11.7 %collective-permute-done.15.refs_1_.refs_2_ = bf16[32,4096]{1,0:T(8,128)(2,1)S(1)} collective-permute-done((bf16[32,4096]{1,0:T(8,128)(2,1)S(1)}, bf16[32,4096]{1,0:T(8,128)(2,1)S(1)}, u32[]{:S(2)}, u32[]{:S(2)}) %collective-permute-start.15) | collective-permute-done | bytes 262176 | tf_op jit(solution)/shard_map/ppermute | solution.py:40
  65.2 1.1 %collective-permute-start.18 = (bf16[64,4096]{1,0:T(8,128)(2,1)S(1)}, bf16[64,4096]{1,0:T(8,128)(2,1)S(1)}, u32[]{:S(2)}, u32[]{:S(2)}) collective-permute-start(bf16[64,4096]{1,0:T(8,128)(2,1)S(1)} %join.10.refs_4_), channel_id=1, source_target_pairs={{0,64},{8,72},{16,80},{24,88},{32,96},{40,104},{48,112},{56,120},{... | collective-permute-start | bytes 1572872 | tf_op jit(solution)/shard_map/ppermute | solution.py:40
  66.3 1.1 %collective-permute-start.19 = (bf16[64,4096]{1,0:T(8,128)(2,1)S(1)}, bf16[64,4096]{1,0:T(8,128)(2,1)S(1)}, u32[]{:S(2)}, u32[]{:S(2)}) collective-permute-start(bf16[64,4096]{1,0:T(8,128)(2,1)S(1)} %join.11.refs_5_), channel_id=1, source_target_pairs={{0,192},{8,200},{16,208},{24,216},{32,224},{40,232},{48,240},{56,2... | collective-permute-start | bytes 1572872 | tf_op jit(solution)/shard_map/ppermute | solution.py:40
  67.4 0.1 join.12
  67.6 1.3 %convolution_convert_fusion = bf16[256,512]{1,0:T(8,128)(2,1)S(1)} fusion(bf16[256,4096]{1,0:T(8,128)(2,1)S(1)} %join.12, bf16[512,4096]{1,0:T(8,128)(2,1)S(1)} %held.1.refs_2_), kind=kOutput, calls=%fused_computation | convolution fusion | flops 1073872896 | bytes 6553600 | tf_op jit(solution)/shard_map/dot_general | solution.py:252
  68.9 0.1 collective-permute-start.17
  69.0 1.3 %convolution_convert_fusion.1.refs_2_ = bf16[256,512]{1,0:T(8,128)(2,1)S(1)} fusion(bf16[256,4096]{1,0:T(8,128)(2,1)S(1)} %join.12, bf16[1,512,4096]{2,1,0:T(8,128)(2,1)S(1)} %copy-done.4), kind=kOutput, calls=%fused_computation.1 | convolution fusion | flops 1073872896 | bytes 6553600 | tf_op jit(solution)/shard_map/dot_general | solution.py:252
  70.3 5.7 %collective-permute-done.18.refs_0_ = bf16[64,4096]{1,0:T(8,128)(2,1)S(1)} collective-permute-done((bf16[64,4096]{1,0:T(8,128)(2,1)S(1)}, bf16[64,4096]{1,0:T(8,128)(2,1)S(1)}, u32[]{:S(2)}, u32[]{:S(2)}) %collective-permute-start.18) | collective-permute-done | bytes 524320 | tf_op jit(solution)/shard_map/ppermute | solution.py:40
  75.9 2.1 %collective-permute-done.19.refs_1_ = bf16[64,4096]{1,0:T(8,128)(2,1)S(1)} collective-permute-done((bf16[64,4096]{1,0:T(8,128)(2,1)S(1)}, bf16[64,4096]{1,0:T(8,128)(2,1)S(1)}, u32[]{:S(2)}, u32[]{:S(2)}) %collective-permute-start.19) | collective-permute-done | bytes 524320 | tf_op jit(solution)/shard_map/ppermute | solution.py:40
  78.0 0.1 join.13
  78.0 1.6 %convolution_convert_fusion.2 = bf16[128,512]{1,0:T(8,128)(2,1)S(1)} fusion(bf16[128,4096]{1,0:T(8,128)(2,1)S(1)} %join.13, bf16[512,4096]{1,0:T(8,128)(2,1)S(1)} %held.1.refs_2_), kind=kOutput, calls=%fused_computation.2 | convolution fusion | flops 536936448 | bytes 5373952 | tf_op jit(solution)/shard_map/dot_general | solution.py:252
  79.6 0.3 collective-permute-start.20
  79.9 1.5 %convolution_convert_fusion.3.refs_4_ = bf16[128,512]{1,0:T(8,128)(2,1)S(1)} fusion(bf16[128,4096]{1,0:T(8,128)(2,1)S(1)} %join.13, bf16[1,512,4096]{2,1,0:T(8,128)(2,1)S(1)} %copy-done.4), kind=kOutput, calls=%fused_computation.3 | convolution fusion | flops 536936448 | bytes 5373952 | tf_op jit(solution)/shard_map/dot_general | solution.py:252
  81.5 0.7 arrange.1
  82.2 0.1 fusion.3
  82.3 0.1 collective-permute-start.21
  82.4 1.6 %collective-permute-start.22 = (bf16[128,512]{1,0:T(8,128)(2,1)S(1)}, bf16[128,512]{1,0:T(8,128)(2,1)S(1)}, u32[]{:S(2)}, u32[]{:S(2)}) collective-permute-start(bf16[128,512]{1,0:T(8,128)(2,1)S(1)} %bitcast.43), channel_id=1, source_target_pairs={{0,1},{1,2},{2,3},{3,0},{4,5},{5,6},{6,7},{7,4},{8,9},{9,10},{10,1... | collective-permute-start | bytes 393224 | tf_op jit(solution)/shard_map/ppermute | solution.py:308
  83.9 4.1 %collective-permute-start.23 = (bf16[128,512]{1,0:T(8,128)(2,1)S(1)}, bf16[128,512]{1,0:T(8,128)(2,1)S(1)}, u32[]{:S(2)}, u32[]{:S(2)}) collective-permute-start(bf16[128,512]{1,0:T(8,128)(2,1)S(1)} %bitcast.42), channel_id=1, source_target_pairs={{0,6},{1,7},{2,4},{3,5},{4,2},{5,3},{6,0},{7,1},{8,14},{9,15},{10,... | collective-permute-start | bytes 393224 | tf_op jit(solution)/shard_map/ppermute | solution.py:308
  88.1 0.8 collective-permute-start.24
  88.9 1.0 collective-permute-start.25
  89.9 3.1 %collective-permute-start.26 = (bf16[128,512]{1,0:T(8,128)(2,1)S(1)}, bf16[128,512]{1,0:T(8,128)(2,1)S(1)}, u32[]{:S(2)}, u32[]{:S(2)}) collective-permute-start(bf16[128,512]{1,0:T(8,128)(2,1)S(1)} %bitcast.39), channel_id=1, source_target_pairs={{0,7},{1,4},{2,5},{3,6},{4,3},{5,0},{6,1},{7,2},{8,15},{9,12},{10,... | collective-permute-start | bytes 393224 | tf_op jit(solution)/shard_map/ppermute | solution.py:308
  93.0 0.5 collective-permute-start.27
  93.5 0.8 collective-permute-done.23.refs_3_
  94.3 5.0 %collective-permute-done.24.refs_4_ = bf16[128,512]{1,0:T(8,128)(2,1)S(1)} collective-permute-done((bf16[128,512]{1,0:T(8,128)(2,1)S(1)}, bf16[128,512]{1,0:T(8,128)(2,1)S(1)}, u32[]{:S(2)}, u32[]{:S(2)}) %collective-permute-start.24) | collective-permute-done | bytes 131104 | tf_op jit(solution)/shard_map/ppermute | solution.py:308
  99.3 1.2 %collective-permute-done.27.refs_7_ = bf16[128,512]{1,0:T(8,128)(2,1)S(1)} collective-permute-done((bf16[128,512]{1,0:T(8,128)(2,1)S(1)}, bf16[128,512]{1,0:T(8,128)(2,1)S(1)}, u32[]{:S(2)}, u32[]{:S(2)}) %collective-permute-start.27) | collective-permute-done | bytes 131104 | tf_op jit(solution)/shard_map/ppermute | solution.py:308
  100.4 0.8 finish.1
  (25 shorter events, 0.2 us)
Async XLA Ops:
  0.0 47.5 %collective-permute-start.11 = (bf16[512,4096]{1,0:T(8,128)(2,1)}, bf16[512,4096]{1,0:T(8,128)(2,1)}, u32[]{:S(2)}, u32[]{:S(2)}) collective-permute-start(bf16[512,4096]{1,0:T(8,128)(2,1)} %bitcast.37), channel_id=1, source_target_pairs={{0,8},{8,0},{16,24},{24,16},{32,40},{40,32},{48,56},{56,48},{64,72... | collective-permute-start | bytes 12582920 | tf_op jit(solution)/shard_map/ppermute | solution.py:40
  0.0 18.2 %collective-permute-start.4 = (bf16[32,4096]{1,0:T(8,128)(2,1)}, bf16[32,4096]{1,0:T(8,128)(2,1)S(1)}, u32[]{:S(2)}, u32[]{:S(2)}) collective-permute-start(bf16[32,4096]{1,0:T(8,128)(2,1)} %bitcast.31), channel_id=1, source_target_pairs={{0,16},{8,24},{16,32},{24,40},{32,48},{40,56},{48,0},{56,8},{64,80... | collective-permute-start | bytes 786440 | tf_op jit(solution)/shard_map/ppermute | solution.py:40
  3.3 17.0 %collective-permute-start.5 = (bf16[32,4096]{1,0:T(8,128)(2,1)}, bf16[32,4096]{1,0:T(8,128)(2,1)S(1)}, u32[]{:S(2)}, u32[]{:S(2)}) collective-permute-start(bf16[32,4096]{1,0:T(8,128)(2,1)} %bitcast.32), channel_id=1, source_target_pairs={{0,48},{8,56},{16,0},{24,8},{32,16},{40,24},{48,32},{56,40},{64,11... | collective-permute-start | bytes 786440 | tf_op jit(solution)/shard_map/ppermute | solution.py:40
  6.4 0.7 copy-start.1
  7.1 0.7 copy-start.2
  7.7 0.7 copy-start.3
  8.4 1.3 %collective-permute-start = (f32[8,128]{1,0:T(8,128)S(1)}, f32[8,128]{1,0:T(8,128)S(1)}, u32[]{:S(2)}, u32[]{:S(2)}) collective-permute-start(f32[8,128]{1,0:T(8,128)S(1)} %pack.1.refs_0_), channel_id=1, source_target_pairs={{0,8},{8,0},{16,24},{24,16},{32,40},{40,32},{48,56},{56,48},{64,72... | collective-permute-start | bytes 12296 | tf_op jit(solution)/shard_map/ppermute | solution.py:40
  9.7 3.7 %collective-permute-start.1 = (f32[16,128]{1,0:T(8,128)S(1)}, f32[16,128]{1,0:T(8,128)S(1)}, u32[]{:S(2)}, u32[]{:S(2)}) collective-permute-start(f32[16,128]{1,0:T(8,128)S(1)} %join.7.refs_0_), channel_id=1, source_target_pairs={{0,64},{8,72},{16,80},{24,88},{32,96},{40,104},{48,112},{56,120},{... | collective-permute-start | bytes 24584 | tf_op jit(solution)/shard_map/ppermute | solution.py:40
  9.9 5.2 %collective-permute-start.2 = (f32[16,128]{1,0:T(8,128)S(1)}, f32[16,128]{1,0:T(8,128)S(1)}, u32[]{:S(2)}, u32[]{:S(2)}) collective-permute-start(f32[16,128]{1,0:T(8,128)S(1)} %join.7.refs_0_), channel_id=1, source_target_pairs={{0,128},{8,136},{16,144},{24,152},{32,160},{40,168},{48,176},{56,1... | collective-permute-start | bytes 24584 | tf_op jit(solution)/shard_map/ppermute | solution.py:40
  13.3 4.9 %collective-permute-start.3 = (f32[16,128]{1,0:T(8,128)S(1)}, f32[16,128]{1,0:T(8,128)S(1)}, u32[]{:S(2)}, u32[]{:S(2)}) collective-permute-start(f32[16,128]{1,0:T(8,128)S(1)} %join.7.refs_0_), channel_id=1, source_target_pairs={{0,192},{8,200},{16,208},{24,216},{32,224},{40,232},{48,240},{56,2... | collective-permute-start | bytes 24584 | tf_op jit(solution)/shard_map/ppermute | solution.py:40
  20.3 7.8 %collective-permute-start.6 = (f32[64,128]{1,0:T(8,128)S(1)}, f32[64,128]{1,0:T(8,128)S(1)}, u32[]{:S(2)}, u32[]{:S(2)}) collective-permute-start(f32[64,128]{1,0:T(8,128)S(1)} %join.8.refs_0_), channel_id=1, source_target_pairs={{0,16},{8,24},{16,32},{24,40},{32,48},{40,56},{48,0},{56,8},{64,80... | collective-permute-start | bytes 98312 | tf_op jit(solution)/shard_map/ppermute | solution.py:40
  24.1 8.1 %collective-permute-start.7 = (f32[64,128]{1,0:T(8,128)S(1)}, f32[64,128]{1,0:T(8,128)S(1)}, u32[]{:S(2)}, u32[]{:S(2)}) collective-permute-start(f32[64,128]{1,0:T(8,128)S(1)} %join.8.refs_0_), channel_id=1, source_target_pairs={{0,32},{8,40},{16,48},{24,56},{32,0},{40,8},{48,16},{56,24},{64,96... | collective-permute-start | bytes 98312 | tf_op jit(solution)/shard_map/ppermute | solution.py:40
  25.3 11.8 %collective-permute-start.8 = (f32[64,128]{1,0:T(8,128)S(1)}, f32[64,128]{1,0:T(8,128)S(1)}, u32[]{:S(2)}, u32[]{:S(2)}) collective-permute-start(f32[64,128]{1,0:T(8,128)S(1)} %join.8.refs_0_), channel_id=1, source_target_pairs={{0,48},{8,56},{16,0},{24,8},{32,16},{40,24},{48,32},{56,40},{64,11... | collective-permute-start | bytes 98312 | tf_op jit(solution)/shard_map/ppermute | solution.py:40
  32.2 11.8 %collective-permute-start.9 = (bf16[16,4096]{1,0:T(8,128)(2,1)S(1)}, bf16[16,4096]{1,0:T(8,128)(2,1)S(1)}, u32[]{:S(2)}, u32[]{:S(2)}) collective-permute-start(bf16[16,4096]{1,0:T(8,128)(2,1)S(1)} %get-tuple-element.17.refs_3_), channel_id=1, source_target_pairs={{0,16},{8,24},{16,32},{24,40},{32,48},{40,56},{48,0},{56,8},{64,80... | collective-permute-start | bytes 393224 | tf_op jit(solution)/shard_map/ppermute | solution.py:40
  32.5 11.5 %collective-permute-start.10 = (bf16[16,4096]{1,0:T(8,128)(2,1)S(1)}, bf16[16,4096]{1,0:T(8,128)(2,1)S(1)}, u32[]{:S(2)}, u32[]{:S(2)}) collective-permute-start(bf16[16,4096]{1,0:T(8,128)(2,1)S(1)} %get-tuple-element.18), channel_id=1, source_target_pairs={{0,48},{8,56},{16,0},{24,8},{32,16},{40,24},{48,32},{56,40},{64,11... | collective-permute-start | bytes 393224 | tf_op jit(solution)/shard_map/ppermute | solution.py:40
  38.3 1.0 copy-start
  41.9 23.3 %collective-permute-start.13 = (bf16[96,4096]{1,0:T(8,128)(2,1)S(1)}, bf16[96,4096]{1,0:T(8,128)(2,1)S(1)}, u32[]{:S(2)}, u32[]{:S(2)}) collective-permute-start(bf16[96,4096]{1,0:T(8,128)(2,1)S(1)} %rotate.2.refs_2_.refs_0_), channel_id=1, source_target_pairs={{0,64},{8,72},{16,80},{24,88},{32,96},{40,104},{48,112},{56,120},{... | collective-permute-start | bytes 2359304 | tf_op jit(solution)/shard_map/ppermute | solution.py:40
  42.2 24.1 %collective-permute-start.14 = (bf16[96,4096]{1,0:T(8,128)(2,1)S(1)}, bf16[96,4096]{1,0:T(8,128)(2,1)S(1)}, u32[]{:S(2)}, u32[]{:S(2)}) collective-permute-start(bf16[96,4096]{1,0:T(8,128)(2,1)S(1)} %rotate.2.refs_2_.refs_0_), channel_id=1, source_target_pairs={{0,192},{8,200},{16,208},{24,216},{32,224},{40,232},{48,240},{56,2... | collective-permute-start | bytes 2359304 | tf_op jit(solution)/shard_map/ppermute | solution.py:40
  45.4 19.8 %collective-permute-start.15 = (bf16[32,4096]{1,0:T(8,128)(2,1)S(1)}, bf16[32,4096]{1,0:T(8,128)(2,1)S(1)}, u32[]{:S(2)}, u32[]{:S(2)}) collective-permute-start(bf16[32,4096]{1,0:T(8,128)(2,1)S(1)} %rotate.3.refs_0_.refs_1_), channel_id=1, source_target_pairs={{0,64},{8,72},{16,80},{24,88},{32,96},{40,104},{48,112},{56,120},{... | collective-permute-start | bytes 786440 | tf_op jit(solution)/shard_map/ppermute | solution.py:40
  47.0 20.5 %collective-permute-start.16 = (bf16[32,4096]{1,0:T(8,128)(2,1)S(1)}, bf16[32,4096]{1,0:T(8,128)(2,1)S(1)}, u32[]{:S(2)}, u32[]{:S(2)}) collective-permute-start(bf16[32,4096]{1,0:T(8,128)(2,1)S(1)} %rotate.3.refs_0_.refs_1_), channel_id=1, source_target_pairs={{0,192},{8,200},{16,208},{24,216},{32,224},{40,232},{48,240},{56,2... | collective-permute-start | bytes 786440 | tf_op jit(solution)/shard_map/ppermute | solution.py:40
  49.8 2.2 %copy-start.4 = (bf16[1,512,4096]{2,1,0:T(8,128)(2,1)S(1)}, bf16[1,512,4096]{2,1,0:T(8,128)(2,1)}, u32[]{:S(2)}) copy-start(bf16[1,512,4096]{2,1,0:T(8,128)(2,1)} %param.7) | copy-start | bytes 12582916
  51.4 30.1 %collective-permute-start.12 = (bf16[128,512]{1,0:T(8,128)(2,1)S(1)}, bf16[128,512]{1,0:T(8,128)(2,1)S(1)}, u32[]{:S(2)}, u32[]{:S(2)}) collective-permute-start(bf16[128,512]{1,0:T(8,128)(2,1)S(1)} %convolution_convert_fusion.4), channel_id=1, source_target_pairs={{0,8},{8,0},{16,24},{24,16},{32,40},{40,32},{48,56},{56,48},{64,72... | collective-permute-start | bytes 393224 | tf_op jit(solution)/shard_map/ppermute | solution.py:40
  65.2 10.7 %collective-permute-start.18 = (bf16[64,4096]{1,0:T(8,128)(2,1)S(1)}, bf16[64,4096]{1,0:T(8,128)(2,1)S(1)}, u32[]{:S(2)}, u32[]{:S(2)}) collective-permute-start(bf16[64,4096]{1,0:T(8,128)(2,1)S(1)} %join.10.refs_4_), channel_id=1, source_target_pairs={{0,64},{8,72},{16,80},{24,88},{32,96},{40,104},{48,112},{56,120},{... | collective-permute-start | bytes 1572872 | tf_op jit(solution)/shard_map/ppermute | solution.py:40
  66.3 11.6 %collective-permute-start.19 = (bf16[64,4096]{1,0:T(8,128)(2,1)S(1)}, bf16[64,4096]{1,0:T(8,128)(2,1)S(1)}, u32[]{:S(2)}, u32[]{:S(2)}) collective-permute-start(bf16[64,4096]{1,0:T(8,128)(2,1)S(1)} %join.11.refs_5_), channel_id=1, source_target_pairs={{0,192},{8,200},{16,208},{24,216},{32,224},{40,232},{48,240},{56,2... | collective-permute-start | bytes 1572872 | tf_op jit(solution)/shard_map/ppermute | solution.py:40
  68.9 12.6 %collective-permute-start.17 = (bf16[256,512]{1,0:T(8,128)(2,1)S(1)}, bf16[256,512]{1,0:T(8,128)(2,1)S(1)}, u32[]{:S(2)}, u32[]{:S(2)}) collective-permute-start(bf16[256,512]{1,0:T(8,128)(2,1)S(1)} %convolution_convert_fusion), channel_id=1, source_target_pairs={{0,8},{8,0},{16,24},{24,16},{32,40},{40,32},{48,56},{56,48},{64,72... | collective-permute-start | bytes 786440 | tf_op jit(solution)/shard_map/ppermute | solution.py:40
  79.6 1.9 %collective-permute-start.20 = (bf16[128,512]{1,0:T(8,128)(2,1)S(1)}, bf16[128,512]{1,0:T(8,128)(2,1)S(1)}, u32[]{:S(2)}, u32[]{:S(2)}) collective-permute-start(bf16[128,512]{1,0:T(8,128)(2,1)S(1)} %convolution_convert_fusion.2), channel_id=1, source_target_pairs={{0,8},{8,0},{16,24},{24,16},{32,40},{40,32},{48,56},{56,48},{64,72... | collective-permute-start | bytes 393224 | tf_op jit(solution)/shard_map/ppermute | solution.py:40
  82.3 7.6 %collective-permute-start.21 = (bf16[128,512]{1,0:T(8,128)(2,1)S(1)}, bf16[128,512]{1,0:T(8,128)(2,1)S(1)}, u32[]{:S(2)}, u32[]{:S(2)}) collective-permute-start(bf16[128,512]{1,0:T(8,128)(2,1)S(1)} %bitcast.44), channel_id=1, source_target_pairs={{0,4},{1,5},{2,6},{3,7},{4,0},{5,1},{6,2},{7,3},{8,12},{9,13},{10,... | collective-permute-start | bytes 393224 | tf_op jit(solution)/shard_map/ppermute | solution.py:308
  82.4 10.6 %collective-permute-start.22 = (bf16[128,512]{1,0:T(8,128)(2,1)S(1)}, bf16[128,512]{1,0:T(8,128)(2,1)S(1)}, u32[]{:S(2)}, u32[]{:S(2)}) collective-permute-start(bf16[128,512]{1,0:T(8,128)(2,1)S(1)} %bitcast.43), channel_id=1, source_target_pairs={{0,1},{1,2},{2,3},{3,0},{4,5},{5,6},{6,7},{7,4},{8,9},{9,10},{10,1... | collective-permute-start | bytes 393224 | tf_op jit(solution)/shard_map/ppermute | solution.py:308
  83.9 10.3 %collective-permute-start.23 = (bf16[128,512]{1,0:T(8,128)(2,1)S(1)}, bf16[128,512]{1,0:T(8,128)(2,1)S(1)}, u32[]{:S(2)}, u32[]{:S(2)}) collective-permute-start(bf16[128,512]{1,0:T(8,128)(2,1)S(1)} %bitcast.42), channel_id=1, source_target_pairs={{0,6},{1,7},{2,4},{3,5},{4,2},{5,3},{6,0},{7,1},{8,14},{9,15},{10,... | collective-permute-start | bytes 393224 | tf_op jit(solution)/shard_map/ppermute | solution.py:308
  88.1 11.2 %collective-permute-start.24 = (bf16[128,512]{1,0:T(8,128)(2,1)S(1)}, bf16[128,512]{1,0:T(8,128)(2,1)S(1)}, u32[]{:S(2)}, u32[]{:S(2)}) collective-permute-start(bf16[128,512]{1,0:T(8,128)(2,1)S(1)} %bitcast.41), channel_id=1, source_target_pairs={{0,2},{1,3},{2,0},{3,1},{4,6},{5,7},{6,4},{7,5},{8,10},{9,11},{10,... | collective-permute-start | bytes 393224 | tf_op jit(solution)/shard_map/ppermute | solution.py:308
  88.9 10.4 %collective-permute-start.25 = (bf16[128,512]{1,0:T(8,128)(2,1)S(1)}, bf16[128,512]{1,0:T(8,128)(2,1)S(1)}, u32[]{:S(2)}, u32[]{:S(2)}) collective-permute-start(bf16[128,512]{1,0:T(8,128)(2,1)S(1)} %bitcast.40), channel_id=1, source_target_pairs={{0,5},{1,6},{2,7},{3,4},{4,1},{5,2},{6,3},{7,0},{8,13},{9,14},{10,... | collective-permute-start | bytes 393224 | tf_op jit(solution)/shard_map/ppermute | solution.py:308
  89.9 9.4 %collective-permute-start.26 = (bf16[128,512]{1,0:T(8,128)(2,1)S(1)}, bf16[128,512]{1,0:T(8,128)(2,1)S(1)}, u32[]{:S(2)}, u32[]{:S(2)}) collective-permute-start(bf16[128,512]{1,0:T(8,128)(2,1)S(1)} %bitcast.39), channel_id=1, source_target_pairs={{0,7},{1,4},{2,5},{3,6},{4,3},{5,0},{6,1},{7,2},{8,15},{9,12},{10,... | collective-permute-start | bytes 393224 | tf_op jit(solution)/shard_map/ppermute | solution.py:308
  93.0 7.4 %collective-permute-start.27 = (bf16[128,512]{1,0:T(8,128)(2,1)S(1)}, bf16[128,512]{1,0:T(8,128)(2,1)S(1)}, u32[]{:S(2)}, u32[]{:S(2)}) collective-permute-start(bf16[128,512]{1,0:T(8,128)(2,1)S(1)} %bitcast.38), channel_id=1, source_target_pairs={{0,3},{1,0},{2,1},{3,2},{4,7},{5,4},{6,5},{7,6},{8,11},{9,8},{10,9... | collective-permute-start | bytes 393224 | tf_op jit(solution)/shard_map/ppermute | solution.py:308

commit v2 on v0

--- a/solution.py
+++ b/solution.py
@@ -31,9 +31,21 @@
 
 
 def layer_shift(dl, dx):
+    layers = NL * NX
+
+    def place(e, a, x):
+        return e * layers + (a % NL) * NX + x % NX
+
     return [
-        (a * NX + x, ((a + dl) % NL) * NX + (x + dx) % NX) for a in range(NL) for x in range(NX)
+        (place(e, a, x), place(e, a + dl, x + dx * (1 - 2 * (e % NC))))
+        for e in range(NY * NZ * NC)
+        for a in range(NL)
+        for x in range(NX)
     ]
+
+
+def to_layer(x, dl, dx):
+    return lax.ppermute(x, ("example", "layer"), layer_shift(dl, dx))
 
 
 def send(x, dy=0, dz=0, dc=0):
@@ -263,7 +275,8 @@
         for at, (dy, dz) in enumerate(offsets[k // 2]):
             from_z = (z - dz) & 3
             to = ((y - dy) & 3) * 2 + (from_z >> 1)
-            turn = ((to ^ layer) & 4) + ((to - layer) & 3)
+            ahead = ((to - layer) * (1 - 2 * c)) & 3
+            turn = (ahead ^ 2) * 2 + (((to ^ layer) >> 2) & 1)
             out_ref[turn * 4 + (from_z & 1) * 2 + kind] = part[ROWS * at : ROWS * (at + 1), :]
 
 
@@ -303,10 +316,11 @@
 
 def spread_over_layers(ready):
     ready = ready.reshape(NL * NX, 4 * ROWS, ready.shape[-1])
-    parts = [ready[0]]
-    for dl, dx in ((1, 2), (0, 2), (1, 1), (1, 3), (1, 0), (0, 1), (0, 3)):
-        parts.append(lax.ppermute(ready[dl * NX + dx], "layer", layer_shift(dl, dx)))
-    return parts
+    passing = to_layer(ready[0:2], 0, 1)
+    parts = [ready[4], to_layer(ready[5], 1, 0)]
+    parts += [to_layer(ready[2], 0, 3), to_layer(ready[3], 1, 3)]
+    joint = (ready[6:8].astype(F32) + passing.astype(F32)).astype(BF16)
+    return parts + [to_layer(joint[0], 0, 1), to_layer(joint[1], 1, 1)]
 
 
 def halves_kernel(behind_ref, ahead_ref, *refs):

time: 98.1 us -> 95.3 us (0.971)
  waiting for transfers between devices: 35.6 us -> 31.3 us
  starting transfers between devices: 40.3 us -> 42.1 us
    ppermute x7 -> x6, waiting for transfers between devices: 9.42 us -> 5.12 us  [to_layer(): return lax.ppermute(x, ('example', 'layer'), layer_shift(dl, dx))]
    ppermute x7 -> x6, starting transfers between devices: 9.97 us -> 11.7 us  [to_layer(): return lax.ppermute(x, ('example', 'layer'), layer_shift(dl, dx))]
  transfers between devices with their start and end apart: 28 -> 27, of which waited for: 13 -> 12; matrix products, arithmetic and copies ran while one was open for 9% -> 9% of each run, Pallas kernels for 6% -> 6%
where the time goes in v2:
time: 95.3 us; the launch traced here: 95.2 us
  starting transfers between devices  42.1 us (44%)
  waiting for transfers between devices  31.3 us (33%)
  matrix products  8.81 us (9%)
  Pallas kernels  7.36 us (8%)
  local copies, waits for them, and re-layouts  4.55 us (5%)
    ppermute x21, starting transfers between devices, send(): return lax.ppermute(x, 'example', example_shift(dy, dz, dc))  30.3 us
    ppermute x21, waiting for transfers between devices, send(): return lax.ppermute(x, 'example', example_shift(dy, dz, dc))  26.2 us
    ppermute x6, starting transfers between devices, to_layer(): return lax.ppermute(x, ('example', 'layer'), layer_shift(dl, dx))  11.7 us
    dot_general x6, matrix products, scores_of(): lax.dot_general(conditioned, documents, (((1,), (1,)), ((), ())), preferr...  8.81 us
    ppermute x6, waiting for transfers between devices, to_layer(): return lax.ppermute(x, ('example', 'layer'), layer_shift(dl, dx))  5.12 us
    unnamed x14, local copies, waits for them, and re-layouts  4.46 us
    pallas_call x2, Pallas kernels, rotate(): pl.pallas_call(functools.partial(rotate_kernel, CHUNK, len(blocks)), out_...  3.98 us
  transfers between devices with their start and end apart: 27, of which 12 were waited for; matrix products, arithmetic and copies ran while one was open for 9% of the time, Pallas kernels for 6%

profile of v2, /device:TPU:24, one launch (start us, length us, event | category | flops | bytes accessed | tf_op | source)
XLA Modules:
  0.0 95.2 jit_solution(11826402208285756732)
XLA Ops:
  0.0 0.0 collective-permute-start.4
  0.0 3.3 %collective-permute-start.8 = (bf16[32,4096]{1,0:T(8,128)(2,1)}, bf16[32,4096]{1,0:T(8,128)(2,1)S(1)}, u32[]{:S(2)}, u32[]{:S(2)}) collective-permute-start(bf16[32,4096]{1,0:T(8,128)(2,1)} %bitcast.36), channel_id=1, source_target_pairs={{0,16},{8,24},{16,32},{24,40},{32,48},{40,56},{48,0},{56,8},{64,80... | collective-permute-start | bytes 786440 | tf_op jit(solution)/shard_map/ppermute | solution.py:52
  3.4 3.1 %collective-permute-start.9 = (bf16[32,4096]{1,0:T(8,128)(2,1)}, bf16[32,4096]{1,0:T(8,128)(2,1)S(1)}, u32[]{:S(2)}, u32[]{:S(2)}) collective-permute-start(bf16[32,4096]{1,0:T(8,128)(2,1)} %bitcast.37), channel_id=1, source_target_pairs={{0,48},{8,56},{16,0},{24,8},{32,16},{40,24},{48,32},{56,40},{64,11... | collective-permute-start | bytes 786440 | tf_op jit(solution)/shard_map/ppermute | solution.py:52
  6.5 0.7 copy-done.3
  7.2 0.7 copy-done.4
  7.8 0.7 copy-done.5
  8.5 0.2 collective-permute-start
  8.7 1.1 %collective-permute-done.refs_1_ = f32[8,128]{1,0:T(8,128)S(1)} collective-permute-done((f32[8,128]{1,0:T(8,128)S(1)}, f32[8,128]{1,0:T(8,128)S(1)}, u32[]{:S(2)}, u32[]{:S(2)}) %collective-permute-start) | collective-permute-done | bytes 4128 | tf_op jit(solution)/shard_map/ppermute | solution.py:52
  9.8 0.2 collective-permute-start.1
  10.0 2.6 %collective-permute-start.2 = (f32[16,128]{1,0:T(8,128)S(1)}, f32[16,128]{1,0:T(8,128)S(1)}, u32[]{:S(2)}, u32[]{:S(2)}) collective-permute-start(f32[16,128]{1,0:T(8,128)S(1)} %join.7.refs_0_), channel_id=1, source_target_pairs={{0,128},{8,136},{16,144},{24,152},{32,160},{40,168},{48,176},{56,1... | collective-permute-start | bytes 24584 | tf_op jit(solution)/shard_map/ppermute | solution.py:52
  12.6 0.8 collective-permute-done.1.refs_1_
  13.4 0.7 collective-permute-start.3
  14.2 1.0 %collective-permute-done.2.refs_2_ = f32[16,128]{1,0:T(8,128)S(1)} collective-permute-done((f32[16,128]{1,0:T(8,128)S(1)}, f32[16,128]{1,0:T(8,128)S(1)}, u32[]{:S(2)}, u32[]{:S(2)}) %collective-permute-start.2) | collective-permute-done | bytes 8224 | tf_op jit(solution)/shard_map/ppermute | solution.py:52
  15.1 3.1 %collective-permute-done.3.refs_3_ = f32[16,128]{1,0:T(8,128)S(1)} collective-permute-done((f32[16,128]{1,0:T(8,128)S(1)}, f32[16,128]{1,0:T(8,128)S(1)}, u32[]{:S(2)}, u32[]{:S(2)}) %collective-permute-start.3) | collective-permute-done | bytes 8224 | tf_op jit(solution)/shard_map/ppermute | solution.py:52
  18.3 2.0 %copy-done = bf16[512,4096]{1,0:T(8,128)(2,1)} copy-done((bf16[512,4096]{1,0:T(8,128)(2,1)}, bf16[512,4096]{1,0:T(8,128)(2,1)S(1)}, u32[]{:S(2)}) %copy-start) | copy-done | bytes 4194328
  20.3 1.4 %collective-permute-start.5 = (f32[64,128]{1,0:T(8,128)S(1)}, f32[64,128]{1,0:T(8,128)S(1)}, u32[]{:S(2)}, u32[]{:S(2)}) collective-permute-start(f32[64,128]{1,0:T(8,128)S(1)} %join.8.refs_0_), channel_id=1, source_target_pairs={{0,16},{8,24},{16,32},{24,40},{32,48},{40,56},{48,0},{56,8},{64,80... | collective-permute-start | bytes 98312 | tf_op jit(solution)/shard_map/ppermute | solution.py:52
  21.6 4.7 %collective-permute-start.6 = (f32[64,128]{1,0:T(8,128)S(1)}, f32[64,128]{1,0:T(8,128)S(1)}, u32[]{:S(2)}, u32[]{:S(2)}) collective-permute-start(f32[64,128]{1,0:T(8,128)S(1)} %join.8.refs_0_), channel_id=1, source_target_pairs={{0,32},{8,40},{16,48},{24,56},{32,0},{40,8},{48,16},{56,24},{64,96... | collective-permute-start | bytes 98312 | tf_op jit(solution)/shard_map/ppermute | solution.py:52
  26.3 3.0 %collective-permute-start.7 = (f32[64,128]{1,0:T(8,128)S(1)}, f32[64,128]{1,0:T(8,128)S(1)}, u32[]{:S(2)}, u32[]{:S(2)}) collective-permute-start(f32[64,128]{1,0:T(8,128)S(1)} %join.8.refs_0_), channel_id=1, source_target_pairs={{0,48},{8,56},{16,0},{24,8},{32,16},{40,24},{48,32},{56,40},{64,11... | collective-permute-start | bytes 98312 | tf_op jit(solution)/shard_map/ppermute | solution.py:52
  29.3 0.0 collective-permute-done.9.ahead_ref.refs_2_
  29.3 0.0 collective-permute-done.5.refs_1_.refs_0_
  29.3 0.1 collective-permute-done.6.refs_2_.refs_1_
  29.5 4.2 %collective-permute-start.10 = (bf16[16,4096]{1,0:T(8,128)(2,1)S(1)}, bf16[16,4096]{1,0:T(8,128)(2,1)S(1)}, u32[]{:S(2)}, u32[]{:S(2)}) collective-permute-start(bf16[16,4096]{1,0:T(8,128)(2,1)S(1)} %get-tuple-element.17.refs_3_), channel_id=1, source_target_pairs={{0,16},{8,24},{16,32},{24,40},{32,48},{40,56},{48,0},{56,8},{64,80... | collective-permute-start | bytes 393224 | tf_op jit(solution)/shard_map/ppermute | solution.py:52
  33.7 0.0 collective-permute-start.11
  33.7 0.1 pad_add_fusion.place_ref
  34.4 1.2 %prepare.1 = (bf16[512,256]{1,0:T(8,128)(2,1)S(1)}, bf16[512,256]{1,0:T(8,128)(2,1)S(1)}, bf16[256,128]{1,0:T(8,128)(2,1)S(1)}, bf16[256,256]{1,0:T(8,128)(2,1)S(1)}, f32[256,128]{1,0:T(8,128)S(1)}) custom-call(s32[2]{0:T(128)S(1)} %pad_add_fusion.place_ref, f32[1]{0:T(128)S(6)} %copy.7.damp_ref, f32[64,128]{1,0:T(8,128)S(1)} %join.8.refs_0_, ...), custom_call_target="tpu_custom_call" | custom-call | flops 200000000 | bytes 1048576 | tf_op jit(solution)/shard_map/prepare/pallas_call | solution.py:183
  35.6 2.6 %rotate.2.refs_2_.refs_0_ = bf16[96,4096]{1,0:T(8,128)(2,1)S(1)} custom-call(bf16[512,256]{1,0:T(8,128)(2,1)S(1)} %get-tuple-element.12.left_ref, bf16[512,256]{1,0:T(8,128)(2,1)S(1)} %get-tuple-element.13.right_ref, bf16[256,128]{1,0:T(8,128)(2,1)S(1)} %get-tuple-element.14.in_ref, bf16[256,256]{1,0:T(8,128)(2,1)S(1)} %get-tuple-element.15.back_ref, ...), custom_call_target="tpu_custom_call" | custom-call | tf_op jit(solution)/shard_map/rotate/pallas_call | solution.py:252
  38.2 0.3 collective-permute-start.13
  38.5 1.8 %collective-permute-start.14 = (bf16[96,4096]{1,0:T(8,128)(2,1)S(1)}, bf16[96,4096]{1,0:T(8,128)(2,1)S(1)}, u32[]{:S(2)}, u32[]{:S(2)}) collective-permute-start(bf16[96,4096]{1,0:T(8,128)(2,1)S(1)} %rotate.2.refs_2_.refs_0_), channel_id=1, source_target_pairs={{0,192},{8,200},{16,208},{24,216},{32,224},{40,232},{48,240},{56,2... | collective-permute-start | bytes 2359304 | tf_op jit(solution)/shard_map/ppermute | solution.py:52
  40.3 0.2 collective-permute-done.11.refs_1_
  40.6 1.4 %rotate.3.refs_0_.refs_1_ = bf16[32,4096]{1,0:T(8,128)(2,1)S(1)} custom-call(bf16[512,256]{1,0:T(8,128)(2,1)S(1)} %get-tuple-element.12.left_ref, bf16[512,256]{1,0:T(8,128)(2,1)S(1)} %get-tuple-element.13.right_ref, bf16[256,128]{1,0:T(8,128)(2,1)S(1)} %get-tuple-element.14.in_ref, bf16[256,256]{1,0:T(8,128)(2,1)S(1)} %get-tuple-element.15.back_ref, ...), custom_call_target="tpu_custom_call" | custom-call | flops 20000000000 | tf_op jit(solution)/shard_map/rotate/pallas_call | solution.py:252
  42.0 1.3 %collective-permute-start.15 = (bf16[32,4096]{1,0:T(8,128)(2,1)S(1)}, bf16[32,4096]{1,0:T(8,128)(2,1)S(1)}, u32[]{:S(2)}, u32[]{:S(2)}) collective-permute-start(bf16[32,4096]{1,0:T(8,128)(2,1)S(1)} %rotate.3.refs_0_.refs_1_), channel_id=1, source_target_pairs={{0,64},{8,72},{16,80},{24,88},{32,96},{40,104},{48,112},{56,120},{... | collective-permute-start | bytes 786440 | tf_op jit(solution)/shard_map/ppermute | solution.py:52
  43.3 0.8 collective-permute-start.16
  44.1 0.3 held.1.refs_2_
  44.3 0.1 join.9
  44.4 0.0 copy-start.6
  44.4 1.6 %convolution_convert_fusion.4 = bf16[128,512]{1,0:T(8,128)(2,1)S(1)} fusion(bf16[128,4096]{1,0:T(8,128)(2,1)S(1)} %join.9, bf16[512,4096]{1,0:T(8,128)(2,1)S(1)} %held.1.refs_2_), kind=kOutput, calls=%fused_computation.4 | convolution fusion | flops 536936448 | bytes 5373952 | tf_op jit(solution)/shard_map/dot_general | solution.py:264
  46.0 0.1 collective-permute-start.12
  46.1 0.5 copy-done.6
  46.6 1.5 %convolution_convert_fusion.5.refs_6_.refs_0_ = bf16[128,512]{1,0:T(8,128)(2,1)S(1)} fusion(bf16[128,4096]{1,0:T(8,128)(2,1)S(1)} %join.9, bf16[1,512,4096]{2,1,0:T(8,128)(2,1)S(1)} %copy-done.6), kind=kOutput, calls=%fused_computation.5 | convolution fusion | flops 536936448 | bytes 5373952 | tf_op jit(solution)/shard_map/dot_general | solution.py:264
  48.2 13.4 %collective-permute-done.15.refs_1_.refs_2_ = bf16[32,4096]{1,0:T(8,128)(2,1)S(1)} collective-permute-done((bf16[32,4096]{1,0:T(8,128)(2,1)S(1)}, bf16[32,4096]{1,0:T(8,128)(2,1)S(1)}, u32[]{:S(2)}, u32[]{:S(2)}) %collective-permute-start.15) | collective-permute-done | bytes 262176 | tf_op jit(solution)/shard_map/ppermute | solution.py:52
  61.6 0.4 collective-permute-start.18
  62.0 1.8 %collective-permute-start.19 = (bf16[64,4096]{1,0:T(8,128)(2,1)S(1)}, bf16[64,4096]{1,0:T(8,128)(2,1)S(1)}, u32[]{:S(2)}, u32[]{:S(2)}) collective-permute-start(bf16[64,4096]{1,0:T(8,128)(2,1)S(1)} %join.11.refs_5_), channel_id=1, source_target_pairs={{0,192},{8,200},{16,208},{24,216},{32,224},{40,232},{48,240},{56,2... | collective-permute-start | bytes 1572872 | tf_op jit(solution)/shard_map/ppermute | solution.py:52
  63.8 0.1 join.12
  63.9 1.3 %convolution_convert_fusion = bf16[256,512]{1,0:T(8,128)(2,1)S(1)} fusion(bf16[256,4096]{1,0:T(8,128)(2,1)S(1)} %join.12, bf16[512,4096]{1,0:T(8,128)(2,1)S(1)} %held.1.refs_2_), kind=kOutput, calls=%fused_computation | convolution fusion | flops 1073872896 | bytes 6553600 | tf_op jit(solution)/shard_map/dot_general | solution.py:264
  65.2 0.1 collective-permute-start.17
  65.3 1.3 %convolution_convert_fusion.1.refs_2_ = bf16[256,512]{1,0:T(8,128)(2,1)S(1)} fusion(bf16[256,4096]{1,0:T(8,128)(2,1)S(1)} %join.12, bf16[1,512,4096]{2,1,0:T(8,128)(2,1)S(1)} %copy-done.6), kind=kOutput, calls=%fused_computation.1 | convolution fusion | flops 1073872896 | bytes 6553600 | tf_op jit(solution)/shard_map/dot_general | solution.py:264
  66.6 5.0 %collective-permute-done.18.refs_0_ = bf16[64,4096]{1,0:T(8,128)(2,1)S(1)} collective-permute-done((bf16[64,4096]{1,0:T(8,128)(2,1)S(1)}, bf16[64,4096]{1,0:T(8,128)(2,1)S(1)}, u32[]{:S(2)}, u32[]{:S(2)}) %collective-permute-start.18) | collective-permute-done | bytes 524320 | tf_op jit(solution)/shard_map/ppermute | solution.py:52
  71.6 1.5 %collective-permute-done.19.refs_1_ = bf16[64,4096]{1,0:T(8,128)(2,1)S(1)} collective-permute-done((bf16[64,4096]{1,0:T(8,128)(2,1)S(1)}, bf16[64,4096]{1,0:T(8,128)(2,1)S(1)}, u32[]{:S(2)}, u32[]{:S(2)}) %collective-permute-start.19) | collective-permute-done | bytes 524320 | tf_op jit(solution)/shard_map/ppermute | solution.py:52
  73.1 0.1 join.13
  73.1 1.6 %convolution_convert_fusion.2 = bf16[128,512]{1,0:T(8,128)(2,1)S(1)} fusion(bf16[128,4096]{1,0:T(8,128)(2,1)S(1)} %join.13, bf16[512,4096]{1,0:T(8,128)(2,1)S(1)} %held.1.refs_2_), kind=kOutput, calls=%fused_computation.2 | convolution fusion | flops 536936448 | bytes 5373952 | tf_op jit(solution)/shard_map/dot_general | solution.py:264
  74.7 0.3 collective-permute-start.20
  75.0 1.5 %convolution_convert_fusion.3.refs_4_ = bf16[128,512]{1,0:T(8,128)(2,1)S(1)} fusion(bf16[128,4096]{1,0:T(8,128)(2,1)S(1)} %join.13, bf16[1,512,4096]{2,1,0:T(8,128)(2,1)S(1)} %copy-done.6), kind=kOutput, calls=%fused_computation.3 | convolution fusion | flops 536936448 | bytes 5373952 | tf_op jit(solution)/shard_map/dot_general | solution.py:264
  76.6 0.7 arrange.1
  77.4 1.6 %collective-permute-start.24 = (bf16[2,128,512]{2,1,0:T(8,128)(2,1)S(1)}, bf16[2,128,512]{2,1,0:T(8,128)(2,1)S(1)}, u32[]{:S(2)}, u32[]{:S(2)}) collective-permute-start(bf16[2,128,512]{2,1,0:T(8,128)(2,1)S(1)} %bitcast.44), channel_id=1, source_target_pairs={{0,1},{1,2},{2,3},{3,0},{4,5},{5,6},{6,7},{7,4},{8,11},{9,8},{10,9... | collective-permute-start | bytes 786440 | tf_op jit(solution)/shard_map/ppermute | solution.py:48
  79.0 1.3 %collective-permute-start.21 = (bf16[128,512]{1,0:T(8,128)(2,1)S(1)}, bf16[128,512]{1,0:T(8,128)(2,1)S(1)}, u32[]{:S(2)}, u32[]{:S(2)}) collective-permute-start(bf16[128,512]{1,0:T(8,128)(2,1)S(1)} %bitcast.47), channel_id=1, source_target_pairs={{0,4},{1,5},{2,6},{3,7},{4,0},{5,1},{6,2},{7,3},{8,12},{9,13},{10,... | collective-permute-start | bytes 393224 | tf_op jit(solution)/shard_map/ppermute | solution.py:48
  80.3 1.7 %collective-permute-start.22 = (bf16[128,512]{1,0:T(8,128)(2,1)S(1)}, bf16[128,512]{1,0:T(8,128)(2,1)S(1)}, u32[]{:S(2)}, u32[]{:S(2)}) collective-permute-start(bf16[128,512]{1,0:T(8,128)(2,1)S(1)} %bitcast.46), channel_id=1, source_target_pairs={{0,3},{1,0},{2,1},{3,2},{4,7},{5,4},{6,5},{7,6},{8,9},{9,10},{10,1... | collective-permute-start | bytes 393224 | tf_op jit(solution)/shard_map/ppermute | solution.py:48
  82.0 1.8 %collective-permute-start.23 = (bf16[128,512]{1,0:T(8,128)(2,1)S(1)}, bf16[128,512]{1,0:T(8,128)(2,1)S(1)}, u32[]{:S(2)}, u32[]{:S(2)}) collective-permute-start(bf16[128,512]{1,0:T(8,128)(2,1)S(1)} %bitcast.45), channel_id=1, source_target_pairs={{0,7},{1,4},{2,5},{3,6},{4,3},{5,0},{6,1},{7,2},{8,13},{9,14},{10,... | collective-permute-start | bytes 393224 | tf_op jit(solution)/shard_map/ppermute | solution.py:48
  83.8 1.2 %collective-permute-done.24 = bf16[2,128,512]{2,1,0:T(8,128)(2,1)S(1)} collective-permute-done((bf16[2,128,512]{2,1,0:T(8,128)(2,1)S(1)}, bf16[2,128,512]{2,1,0:T(8,128)(2,1)S(1)}, u32[]{:S(2)}, u32[]{:S(2)}) %collective-permute-start.24) | collective-permute-done | bytes 262176 | tf_op jit(solution)/shard_map/ppermute | solution.py:48
  85.0 0.1 fusion
  85.1 2.2 %collective-permute-start.25 = (bf16[128,512]{1,0:T(8,128)(2,1)S(1)}, bf16[128,512]{1,0:T(8,128)(2,1)S(1)}, u32[]{:S(2)}, u32[]{:S(2)}) collective-permute-start(bf16[128,512]{1,0:T(8,128)(2,1)S(1)} %get-tuple-element.26), channel_id=1, source_target_pairs={{0,1},{1,2},{2,3},{3,0},{4,5},{5,6},{6,7},{7,4},{8,11},{9,8},{10,9... | collective-permute-start | bytes 393224 | tf_op jit(solution)/shard_map/ppermute | solution.py:48
  87.3 3.2 %collective-permute-start.26 = (bf16[128,512]{1,0:T(8,128)(2,1)S(1)}, bf16[128,512]{1,0:T(8,128)(2,1)S(1)}, u32[]{:S(2)}, u32[]{:S(2)}) collective-permute-start(bf16[128,512]{1,0:T(8,128)(2,1)S(1)} %get-tuple-element.25), channel_id=1, source_target_pairs={{0,5},{1,6},{2,7},{3,4},{4,1},{5,2},{6,3},{7,0},{8,15},{9,12},{10,... | collective-permute-start | bytes 393224 | tf_op jit(solution)/shard_map/ppermute | solution.py:48
  90.5 0.9 collective-permute-done.25.refs_4_
  91.4 3.0 %collective-permute-done.26.refs_5_ = bf16[128,512]{1,0:T(8,128)(2,1)S(1)} collective-permute-done((bf16[128,512]{1,0:T(8,128)(2,1)S(1)}, bf16[128,512]{1,0:T(8,128)(2,1)S(1)}, u32[]{:S(2)}, u32[]{:S(2)}) %collective-permute-start.26) | collective-permute-done | bytes 131104 | tf_op jit(solution)/shard_map/ppermute | solution.py:48
  94.4 0.8 finish.1
  (30 shorter events, 0.3 us)
Async XLA Ops:
  0.0 35.6 %copy-start.2 = (bf16[1,32,4096]{2,1,0:T(8,128)(2,1)S(1)}, bf16[1,32,4096]{2,1,0:T(8,128)(2,1)}, u32[]{:S(2)}) copy-start(bf16[1,32,4096]{2,1,0:T(8,128)(2,1)} %param.6) | copy-start | bytes 786436
  0.0 18.3 %collective-permute-start.4 = (bf16[512,4096]{1,0:T(8,128)(2,1)}, bf16[512,4096]{1,0:T(8,128)(2,1)S(1)}, u32[]{:S(2)}, u32[]{:S(2)}) collective-permute-start(bf16[512,4096]{1,0:T(8,128)(2,1)} %bitcast.42), channel_id=1, source_target_pairs={{0,8},{8,0},{16,24},{24,16},{32,40},{40,32},{48,56},{56,48},{64,72... | collective-permute-start | bytes 12582920 | tf_op jit(solution)/shard_map/ppermute | solution.py:52
  0.0 29.3 %collective-permute-start.8 = (bf16[32,4096]{1,0:T(8,128)(2,1)}, bf16[32,4096]{1,0:T(8,128)(2,1)S(1)}, u32[]{:S(2)}, u32[]{:S(2)}) collective-permute-start(bf16[32,4096]{1,0:T(8,128)(2,1)} %bitcast.36), channel_id=1, source_target_pairs={{0,16},{8,24},{16,32},{24,40},{32,48},{40,56},{48,0},{56,8},{64,80... | collective-permute-start | bytes 786440 | tf_op jit(solution)/shard_map/ppermute | solution.py:52
  3.4 26.0 %collective-permute-start.9 = (bf16[32,4096]{1,0:T(8,128)(2,1)}, bf16[32,4096]{1,0:T(8,128)(2,1)S(1)}, u32[]{:S(2)}, u32[]{:S(2)}) collective-permute-start(bf16[32,4096]{1,0:T(8,128)(2,1)} %bitcast.37), channel_id=1, source_target_pairs={{0,48},{8,56},{16,0},{24,8},{32,16},{40,24},{48,32},{56,40},{64,11... | collective-permute-start | bytes 786440 | tf_op jit(solution)/shard_map/ppermute | solution.py:52
  6.5 0.7 copy-start.3
  7.2 0.7 copy-start.4
  7.8 0.7 copy-start.5
  8.5 1.3 %collective-permute-start = (f32[8,128]{1,0:T(8,128)S(1)}, f32[8,128]{1,0:T(8,128)S(1)}, u32[]{:S(2)}, u32[]{:S(2)}) collective-permute-start(f32[8,128]{1,0:T(8,128)S(1)} %pack.1.refs_0_), channel_id=1, source_target_pairs={{0,8},{8,0},{16,24},{24,16},{32,40},{40,32},{48,56},{56,48},{64,72... | collective-permute-start | bytes 12296 | tf_op jit(solution)/shard_map/ppermute | solution.py:52
  9.8 3.7 %collective-permute-start.1 = (f32[16,128]{1,0:T(8,128)S(1)}, f32[16,128]{1,0:T(8,128)S(1)}, u32[]{:S(2)}, u32[]{:S(2)}) collective-permute-start(f32[16,128]{1,0:T(8,128)S(1)} %join.7.refs_0_), channel_id=1, source_target_pairs={{0,64},{8,72},{16,80},{24,88},{32,96},{40,104},{48,112},{56,120},{... | collective-permute-start | bytes 24584 | tf_op jit(solution)/shard_map/ppermute | solution.py:52
  10.0 5.2 %collective-permute-start.2 = (f32[16,128]{1,0:T(8,128)S(1)}, f32[16,128]{1,0:T(8,128)S(1)}, u32[]{:S(2)}, u32[]{:S(2)}) collective-permute-start(f32[16,128]{1,0:T(8,128)S(1)} %join.7.refs_0_), channel_id=1, source_target_pairs={{0,128},{8,136},{16,144},{24,152},{32,160},{40,168},{48,176},{56,1... | collective-permute-start | bytes 24584 | tf_op jit(solution)/shard_map/ppermute | solution.py:52
  13.4 4.9 %collective-permute-start.3 = (f32[16,128]{1,0:T(8,128)S(1)}, f32[16,128]{1,0:T(8,128)S(1)}, u32[]{:S(2)}, u32[]{:S(2)}) collective-permute-start(f32[16,128]{1,0:T(8,128)S(1)} %join.7.refs_0_), channel_id=1, source_target_pairs={{0,192},{8,200},{16,208},{24,216},{32,224},{40,232},{48,240},{56,2... | collective-permute-start | bytes 24584 | tf_op jit(solution)/shard_map/ppermute | solution.py:52
  18.3 2.0 %copy-start = (bf16[512,4096]{1,0:T(8,128)(2,1)}, bf16[512,4096]{1,0:T(8,128)(2,1)S(1)}, u32[]{:S(2)}) copy-start(bf16[512,4096]{1,0:T(8,128)(2,1)S(1)} %collective-permute-done.4.refs_4_.x_ref) | copy-start | bytes 12582916
  20.3 9.1 %collective-permute-start.5 = (f32[64,128]{1,0:T(8,128)S(1)}, f32[64,128]{1,0:T(8,128)S(1)}, u32[]{:S(2)}, u32[]{:S(2)}) collective-permute-start(f32[64,128]{1,0:T(8,128)S(1)} %join.8.refs_0_), channel_id=1, source_target_pairs={{0,16},{8,24},{16,32},{24,40},{32,48},{40,56},{48,0},{56,8},{64,80... | collective-permute-start | bytes 98312 | tf_op jit(solution)/shard_map/ppermute | solution.py:52
  21.6 7.8 %collective-permute-start.6 = (f32[64,128]{1,0:T(8,128)S(1)}, f32[64,128]{1,0:T(8,128)S(1)}, u32[]{:S(2)}, u32[]{:S(2)}) collective-permute-start(f32[64,128]{1,0:T(8,128)S(1)} %join.8.refs_0_), channel_id=1, source_target_pairs={{0,32},{8,40},{16,48},{24,56},{32,0},{40,8},{48,16},{56,24},{64,96... | collective-permute-start | bytes 98312 | tf_op jit(solution)/shard_map/ppermute | solution.py:52
  26.3 8.1 %collective-permute-start.7 = (f32[64,128]{1,0:T(8,128)S(1)}, f32[64,128]{1,0:T(8,128)S(1)}, u32[]{:S(2)}, u32[]{:S(2)}) collective-permute-start(f32[64,128]{1,0:T(8,128)S(1)} %join.8.refs_0_), channel_id=1, source_target_pairs={{0,48},{8,56},{16,0},{24,8},{32,16},{40,24},{48,32},{56,40},{64,11... | collective-permute-start | bytes 98312 | tf_op jit(solution)/shard_map/ppermute | solution.py:52
  29.5 10.9 %collective-permute-start.10 = (bf16[16,4096]{1,0:T(8,128)(2,1)S(1)}, bf16[16,4096]{1,0:T(8,128)(2,1)S(1)}, u32[]{:S(2)}, u32[]{:S(2)}) collective-permute-start(bf16[16,4096]{1,0:T(8,128)(2,1)S(1)} %get-tuple-element.17.refs_3_), channel_id=1, source_target_pairs={{0,16},{8,24},{16,32},{24,40},{32,48},{40,56},{48,0},{56,8},{64,80... | collective-permute-start | bytes 393224 | tf_op jit(solution)/shard_map/ppermute | solution.py:52
  33.7 6.9 %collective-permute-start.11 = (bf16[16,4096]{1,0:T(8,128)(2,1)S(1)}, bf16[16,4096]{1,0:T(8,128)(2,1)S(1)}, u32[]{:S(2)}, u32[]{:S(2)}) collective-permute-start(bf16[16,4096]{1,0:T(8,128)(2,1)S(1)} %get-tuple-element.18), channel_id=1, source_target_pairs={{0,48},{8,56},{16,0},{24,8},{32,16},{40,24},{48,32},{56,40},{64,11... | collective-permute-start | bytes 393224 | tf_op jit(solution)/shard_map/ppermute | solution.py:52
  38.2 5.8 %copy-start.1 = (bf16[512,4096]{1,0:T(8,128)(2,1)S(1)}, bf16[512,4096]{1,0:T(8,128)(2,1)}, u32[]{:S(2)}) copy-start(bf16[512,4096]{1,0:T(8,128)(2,1)} %copy-done) | copy-start | bytes 12582916
  38.2 23.3 %collective-permute-start.13 = (bf16[96,4096]{1,0:T(8,128)(2,1)S(1)}, bf16[96,4096]{1,0:T(8,128)(2,1)S(1)}, u32[]{:S(2)}, u32[]{:S(2)}) collective-permute-start(bf16[96,4096]{1,0:T(8,128)(2,1)S(1)} %rotate.2.refs_2_.refs_0_), channel_id=1, source_target_pairs={{0,64},{8,72},{16,80},{24,88},{32,96},{40,104},{48,112},{56,120},{... | collective-permute-start | bytes 2359304 | tf_op jit(solution)/shard_map/ppermute | solution.py:52
  38.5 23.4 %collective-permute-start.14 = (bf16[96,4096]{1,0:T(8,128)(2,1)S(1)}, bf16[96,4096]{1,0:T(8,128)(2,1)S(1)}, u32[]{:S(2)}, u32[]{:S(2)}) collective-permute-start(bf16[96,4096]{1,0:T(8,128)(2,1)S(1)} %rotate.2.refs_2_.refs_0_), channel_id=1, source_target_pairs={{0,192},{8,200},{16,208},{24,216},{32,224},{40,232},{48,240},{56,2... | collective-permute-start | bytes 2359304 | tf_op jit(solution)/shard_map/ppermute | solution.py:52
  42.0 19.6 %collective-permute-start.15 = (bf16[32,4096]{1,0:T(8,128)(2,1)S(1)}, bf16[32,4096]{1,0:T(8,128)(2,1)S(1)}, u32[]{:S(2)}, u32[]{:S(2)}) collective-permute-start(bf16[32,4096]{1,0:T(8,128)(2,1)S(1)} %rotate.3.refs_0_.refs_1_), channel_id=1, source_target_pairs={{0,64},{8,72},{16,80},{24,88},{32,96},{40,104},{48,112},{56,120},{... | collective-permute-start | bytes 786440 | tf_op jit(solution)/shard_map/ppermute | solution.py:52
  43.3 20.5 %collective-permute-start.16 = (bf16[32,4096]{1,0:T(8,128)(2,1)S(1)}, bf16[32,4096]{1,0:T(8,128)(2,1)S(1)}, u32[]{:S(2)}, u32[]{:S(2)}) collective-permute-start(bf16[32,4096]{1,0:T(8,128)(2,1)S(1)} %rotate.3.refs_0_.refs_1_), channel_id=1, source_target_pairs={{0,192},{8,200},{16,208},{24,216},{32,224},{40,232},{48,240},{56,2... | collective-permute-start | bytes 786440 | tf_op jit(solution)/shard_map/ppermute | solution.py:52
  44.4 2.2 %copy-start.6 = (bf16[1,512,4096]{2,1,0:T(8,128)(2,1)S(1)}, bf16[1,512,4096]{2,1,0:T(8,128)(2,1)}, u32[]{:S(2)}) copy-start(bf16[1,512,4096]{2,1,0:T(8,128)(2,1)} %param.7) | copy-start | bytes 12582916
  46.0 30.6 %collective-permute-start.12 = (bf16[128,512]{1,0:T(8,128)(2,1)S(1)}, bf16[128,512]{1,0:T(8,128)(2,1)S(1)}, u32[]{:S(2)}, u32[]{:S(2)}) collective-permute-start(bf16[128,512]{1,0:T(8,128)(2,1)S(1)} %convolution_convert_fusion.4), channel_id=1, source_target_pairs={{0,8},{8,0},{16,24},{24,16},{32,40},{40,32},{48,56},{56,48},{64,72... | collective-permute-start | bytes 393224 | tf_op jit(solution)/shard_map/ppermute | solution.py:52
  61.6 10.0 %collective-permute-start.18 = (bf16[64,4096]{1,0:T(8,128)(2,1)S(1)}, bf16[64,4096]{1,0:T(8,128)(2,1)S(1)}, u32[]{:S(2)}, u32[]{:S(2)}) collective-permute-start(bf16[64,4096]{1,0:T(8,128)(2,1)S(1)} %join.10.refs_4_), channel_id=1, source_target_pairs={{0,64},{8,72},{16,80},{24,88},{32,96},{40,104},{48,112},{56,120},{... | collective-permute-start | bytes 1572872 | tf_op jit(solution)/shard_map/ppermute | solution.py:52
  62.0 11.1 %collective-permute-start.19 = (bf16[64,4096]{1,0:T(8,128)(2,1)S(1)}, bf16[64,4096]{1,0:T(8,128)(2,1)S(1)}, u32[]{:S(2)}, u32[]{:S(2)}) collective-permute-start(bf16[64,4096]{1,0:T(8,128)(2,1)S(1)} %join.11.refs_5_), channel_id=1, source_target_pairs={{0,192},{8,200},{16,208},{24,216},{32,224},{40,232},{48,240},{56,2... | collective-permute-start | bytes 1572872 | tf_op jit(solution)/shard_map/ppermute | solution.py:52
  65.2 11.4 %collective-permute-start.17 = (bf16[256,512]{1,0:T(8,128)(2,1)S(1)}, bf16[256,512]{1,0:T(8,128)(2,1)S(1)}, u32[]{:S(2)}, u32[]{:S(2)}) collective-permute-start(bf16[256,512]{1,0:T(8,128)(2,1)S(1)} %convolution_convert_fusion), channel_id=1, source_target_pairs={{0,8},{8,0},{16,24},{24,16},{32,40},{40,32},{48,56},{56,48},{64,72... | collective-permute-start | bytes 786440 | tf_op jit(solution)/shard_map/ppermute | solution.py:52
  74.7 1.9 %collective-permute-start.20 = (bf16[128,512]{1,0:T(8,128)(2,1)S(1)}, bf16[128,512]{1,0:T(8,128)(2,1)S(1)}, u32[]{:S(2)}, u32[]{:S(2)}) collective-permute-start(bf16[128,512]{1,0:T(8,128)(2,1)S(1)} %convolution_convert_fusion.2), channel_id=1, source_target_pairs={{0,8},{8,0},{16,24},{24,16},{32,40},{40,32},{48,56},{56,48},{64,72... | collective-permute-start | bytes 393224 | tf_op jit(solution)/shard_map/ppermute | solution.py:52
  77.4 7.7 %collective-permute-start.24 = (bf16[2,128,512]{2,1,0:T(8,128)(2,1)S(1)}, bf16[2,128,512]{2,1,0:T(8,128)(2,1)S(1)}, u32[]{:S(2)}, u32[]{:S(2)}) collective-permute-start(bf16[2,128,512]{2,1,0:T(8,128)(2,1)S(1)} %bitcast.44), channel_id=1, source_target_pairs={{0,1},{1,2},{2,3},{3,0},{4,5},{5,6},{6,7},{7,4},{8,11},{9,8},{10,9... | collective-permute-start | bytes 786440 | tf_op jit(solution)/shard_map/ppermute | solution.py:48
  79.0 11.5 %collective-permute-start.21 = (bf16[128,512]{1,0:T(8,128)(2,1)S(1)}, bf16[128,512]{1,0:T(8,128)(2,1)S(1)}, u32[]{:S(2)}, u32[]{:S(2)}) collective-permute-start(bf16[128,512]{1,0:T(8,128)(2,1)S(1)} %bitcast.47), channel_id=1, source_target_pairs={{0,4},{1,5},{2,6},{3,7},{4,0},{5,1},{6,2},{7,3},{8,12},{9,13},{10,... | collective-permute-start | bytes 393224 | tf_op jit(solution)/shard_map/ppermute | solution.py:48
  80.3 10.2 %collective-permute-start.22 = (bf16[128,512]{1,0:T(8,128)(2,1)S(1)}, bf16[128,512]{1,0:T(8,128)(2,1)S(1)}, u32[]{:S(2)}, u32[]{:S(2)}) collective-permute-start(bf16[128,512]{1,0:T(8,128)(2,1)S(1)} %bitcast.46), channel_id=1, source_target_pairs={{0,3},{1,0},{2,1},{3,2},{4,7},{5,4},{6,5},{7,6},{8,9},{9,10},{10,1... | collective-permute-start | bytes 393224 | tf_op jit(solution)/shard_map/ppermute | solution.py:48
  82.0 8.4 %collective-permute-start.23 = (bf16[128,512]{1,0:T(8,128)(2,1)S(1)}, bf16[128,512]{1,0:T(8,128)(2,1)S(1)}, u32[]{:S(2)}, u32[]{:S(2)}) collective-permute-start(bf16[128,512]{1,0:T(8,128)(2,1)S(1)} %bitcast.45), channel_id=1, source_target_pairs={{0,7},{1,4},{2,5},{3,6},{4,3},{5,0},{6,1},{7,2},{8,13},{9,14},{10,... | collective-permute-start | bytes 393224 | tf_op jit(solution)/shard_map/ppermute | solution.py:48
  85.1 6.3 %collective-permute-start.25 = (bf16[128,512]{1,0:T(8,128)(2,1)S(1)}, bf16[128,512]{1,0:T(8,128)(2,1)S(1)}, u32[]{:S(2)}, u32[]{:S(2)}) collective-permute-start(bf16[128,512]{1,0:T(8,128)(2,1)S(1)} %get-tuple-element.26), channel_id=1, source_target_pairs={{0,1},{1,2},{2,3},{3,0},{4,5},{5,6},{6,7},{7,4},{8,11},{9,8},{10,9... | collective-permute-start | bytes 393224 | tf_op jit(solution)/shard_map/ppermute | solution.py:48
  87.3 7.1 %collective-permute-start.26 = (bf16[128,512]{1,0:T(8,128)(2,1)S(1)}, bf16[128,512]{1,0:T(8,128)(2,1)S(1)}, u32[]{:S(2)}, u32[]{:S(2)}) collective-permute-start(bf16[128,512]{1,0:T(8,128)(2,1)S(1)} %get-tuple-element.25), channel_id=1, source_target_pairs={{0,5},{1,6},{2,7},{3,4},{4,1},{5,2},{6,3},{7,0},{8,15},{9,12},{10,... | collective-permute-start | bytes 393224 | tf_op jit(solution)/shard_map/ppermute | solution.py:48

commit v3 on v2

--- a/solution.py
+++ b/solution.py
@@ -356,7 +356,7 @@
     row = pack(in_basis[0], eigenvalues[0], out_basis[0])
     pair = join([row, send(row, dc=1)], [])
     column = [send(pair, dy=d) for d in range(1, NY)]
-    plane = join([pair] + column, [docs_there])
+    plane = join([pair] + column, [])
     pieces = [plane] + [send(plane, dz=d) for d in range(1, NZ)]
     tables = prepare(place, damping, pieces, [])
 
@@ -368,22 +368,26 @@
     other = rotate(tables, far, [side], 20_000_000_000)
     other_y = both_ways(other, "dy")
 
-    low = join([side_y[1]], [], [(ROWS, 3 * ROWS)])
-    high = join([side_y[0], other_y[0]], [], [(0, ROWS), (0, ROWS)])
+    docs_other = held(docs_there, [other])
+
+    def scored(blocks, after):
+        conditioned = join(blocks, after)
+        theirs = send(scores_of(conditioned, docs_other), dc=1)
+        return [scores_of(conditioned, docs), theirs]
+
+    parts = scored((side, other), [docs_other])
+
+    low = join([side_y[1]], parts[:1], [(ROWS, 3 * ROWS)])
+    high = join([side_y[0], other_y[0]], parts[:1], [(0, ROWS), (0, ROWS)])
     side_far = send(high, dy=1), send(low, dy=-1)
-
-    docs_other = held(docs_there, [other])
+    parts += scored((*side_y, *other_y), [high, low])
+    parts += scored(side_far, parts[2:3])
 
     offsets = [
         [(0, 0), (0, 1), (0, -1), (0, 2)],
         [(1, 0), (1, 1), (1, -1), (-1, 0), (-1, 1), (-1, -1), (1, 2), (-1, 2)],
         [(2, 0), (2, 2), (2, 1), (2, -1)],
     ]
-    parts = []
-    for blocks, after in (((side, other), [docs_other]), ((*side_y, *other_y), [high, low]), (side_far, [])):
-        conditioned = join(blocks, after + parts[-2:-1])
-        theirs = send(scores_of(conditioned, docs_other), dc=1)
-        parts += [scores_of(conditioned, docs), theirs]
     return finish(spread_over_layers(arrange(place, offsets, parts, [])))
 
 

time: 95.3 us -> 94.3 us (0.990)
  Pallas kernels: 7.36 us -> 9.28 us
  waiting for transfers between devices: 31.3 us -> 29.4 us
  local copies, waits for them, and re-layouts: 4.55 us -> 3.52 us
    ppermute x21, waiting for transfers between devices: 26.2 us -> 24.2 us  [send(): return lax.ppermute(x, 'example', example_shift(dy, dz, dc))]
    pallas_call x1, Pallas kernels: 0.28 us -> 2.19 us  [held(): pl.pallas_call(held_kernel, out_shape=jax.ShapeDtypeStruct(x.shape, x.dty...]
    unnamed x14 -> x10, local copies, waits for them, and re-layouts: 4.46 us -> 3.43 us
  transfers between devices with their start and end apart: 27 -> 27, of which waited for: 12 -> 11; matrix products, arithmetic and copies ran while one was open for 9% -> 10% of each run, Pallas kernels for 6% -> 8%
where the time goes in v3:
time: 94.3 us; the launch traced here: 94.1 us
  starting transfers between devices  42 us (45%)
  waiting for transfers between devices  29.4 us (31%)
  Pallas kernels  9.28 us (10%)
  matrix products  8.8 us (9%)
  local copies, waits for them, and re-layouts  3.52 us (4%)
    ppermute x21, starting transfers between devices, send(): return lax.ppermute(x, 'example', example_shift(dy, dz, dc))  30.4 us
    ppermute x21, waiting for transfers between devices, send(): return lax.ppermute(x, 'example', example_shift(dy, dz, dc))  24.2 us
    ppermute x6, starting transfers between devices, to_layer(): return lax.ppermute(x, ('example', 'layer'), layer_shift(dl, dx))  11.6 us
    dot_general x6, matrix products, scores_of(): lax.dot_general(conditioned, documents, (((1,), (1,)), ((), ())), preferr...  8.8 us
    ppermute x6, waiting for transfers between devices, to_layer(): return lax.ppermute(x, ('example', 'layer'), layer_shift(dl, dx))  5.23 us
    pallas_call x2, Pallas kernels, rotate(): pl.pallas_call(functools.partial(rotate_kernel, CHUNK, len(blocks)), out_...  3.98 us
    unnamed x10, local copies, waits for them, and re-layouts  3.43 us
    pallas_call x1, Pallas kernels, held(): pl.pallas_call(held_kernel, out_shape=jax.ShapeDtypeStruct(x.shape, x.dty...  2.19 us
  transfers between devices with their start and end apart: 27, of which 11 were waited for; matrix products, arithmetic and copies ran while one was open for 10% of the time, Pallas kernels for 8%

profile of v3, /device:TPU:24, one launch (start us, length us, event | category | flops | bytes accessed | tf_op | source)
XLA Modules:
  0.0 94.1 jit_solution(4473886139216574031)
XLA Ops:
  0.0 0.0 collective-permute-start.11
  0.0 3.3 %collective-permute-start.7 = (bf16[32,4096]{1,0:T(8,128)(2,1)}, bf16[32,4096]{1,0:T(8,128)(2,1)S(1)}, u32[]{:S(2)}, u32[]{:S(2)}) collective-permute-start(bf16[32,4096]{1,0:T(8,128)(2,1)} %bitcast.36), channel_id=1, source_target_pairs={{0,16},{8,24},{16,32},{24,40},{32,48},{40,56},{48,0},{56,8},{64,80... | collective-permute-start | bytes 786440 | tf_op jit(solution)/shard_map/ppermute | solution.py:52
  3.3 3.1 %collective-permute-start.8 = (bf16[32,4096]{1,0:T(8,128)(2,1)}, bf16[32,4096]{1,0:T(8,128)(2,1)S(1)}, u32[]{:S(2)}, u32[]{:S(2)}) collective-permute-start(bf16[32,4096]{1,0:T(8,128)(2,1)} %bitcast.37), channel_id=1, source_target_pairs={{0,48},{8,56},{16,0},{24,8},{32,16},{40,24},{48,32},{56,40},{64,11... | collective-permute-start | bytes 786440 | tf_op jit(solution)/shard_map/ppermute | solution.py:52
  6.4 0.7 copy-done.1
  7.1 0.7 copy-done.2
  7.7 0.7 copy-done.3
  8.4 0.2 collective-permute-start
  8.7 1.0 %collective-permute-done.refs_1_ = f32[8,128]{1,0:T(8,128)S(1)} collective-permute-done((f32[8,128]{1,0:T(8,128)S(1)}, f32[8,128]{1,0:T(8,128)S(1)}, u32[]{:S(2)}, u32[]{:S(2)}) %collective-permute-start) | collective-permute-done | bytes 4128 | tf_op jit(solution)/shard_map/ppermute | solution.py:52
  9.7 0.2 collective-permute-start.1
  9.9 2.6 %collective-permute-start.2 = (f32[16,128]{1,0:T(8,128)S(1)}, f32[16,128]{1,0:T(8,128)S(1)}, u32[]{:S(2)}, u32[]{:S(2)}) collective-permute-start(f32[16,128]{1,0:T(8,128)S(1)} %join.7.refs_0_), channel_id=1, source_target_pairs={{0,128},{8,136},{16,144},{24,152},{32,160},{40,168},{48,176},{56,1... | collective-permute-start | bytes 24584 | tf_op jit(solution)/shard_map/ppermute | solution.py:52
  12.5 0.8 collective-permute-done.1.refs_1_
  13.3 0.7 collective-permute-start.3
  14.1 1.0 %collective-permute-done.2.refs_2_ = f32[16,128]{1,0:T(8,128)S(1)} collective-permute-done((f32[16,128]{1,0:T(8,128)S(1)}, f32[16,128]{1,0:T(8,128)S(1)}, u32[]{:S(2)}, u32[]{:S(2)}) %collective-permute-start.2) | collective-permute-done | bytes 8224 | tf_op jit(solution)/shard_map/ppermute | solution.py:52
  15.1 3.1 %collective-permute-done.3.refs_3_ = f32[16,128]{1,0:T(8,128)S(1)} collective-permute-done((f32[16,128]{1,0:T(8,128)S(1)}, f32[16,128]{1,0:T(8,128)S(1)}, u32[]{:S(2)}, u32[]{:S(2)}) %collective-permute-start.3) | collective-permute-done | bytes 8224 | tf_op jit(solution)/shard_map/ppermute | solution.py:52
  18.2 1.4 %collective-permute-start.4 = (f32[64,128]{1,0:T(8,128)S(1)}, f32[64,128]{1,0:T(8,128)S(1)}, u32[]{:S(2)}, u32[]{:S(2)}) collective-permute-start(f32[64,128]{1,0:T(8,128)S(1)} %join.8.refs_0_), channel_id=1, source_target_pairs={{0,16},{8,24},{16,32},{24,40},{32,48},{40,56},{48,0},{56,8},{64,80... | collective-permute-start | bytes 98312 | tf_op jit(solution)/shard_map/ppermute | solution.py:52
  19.6 4.8 %collective-permute-start.5 = (f32[64,128]{1,0:T(8,128)S(1)}, f32[64,128]{1,0:T(8,128)S(1)}, u32[]{:S(2)}, u32[]{:S(2)}) collective-permute-start(f32[64,128]{1,0:T(8,128)S(1)} %join.8.refs_0_), channel_id=1, source_target_pairs={{0,32},{8,40},{16,48},{24,56},{32,0},{40,8},{48,16},{56,24},{64,96... | collective-permute-start | bytes 98312 | tf_op jit(solution)/shard_map/ppermute | solution.py:52
  24.3 0.0 collective-permute-done.4.refs_1_.refs_0_
  24.4 2.9 %collective-permute-start.6 = (f32[64,128]{1,0:T(8,128)S(1)}, f32[64,128]{1,0:T(8,128)S(1)}, u32[]{:S(2)}, u32[]{:S(2)}) collective-permute-start(f32[64,128]{1,0:T(8,128)S(1)} %join.8.refs_0_), channel_id=1, source_target_pairs={{0,48},{8,56},{16,0},{24,8},{32,16},{40,24},{48,32},{56,40},{64,11... | collective-permute-start | bytes 98312 | tf_op jit(solution)/shard_map/ppermute | solution.py:52
  27.3 0.1 collective-permute-done.5.refs_2_.refs_1_
  27.4 0.0 collective-permute-done.7.behind_ref.refs_1_
  27.4 4.2 %collective-permute-start.9 = (bf16[16,4096]{1,0:T(8,128)(2,1)S(1)}, bf16[16,4096]{1,0:T(8,128)(2,1)S(1)}, u32[]{:S(2)}, u32[]{:S(2)}) collective-permute-start(bf16[16,4096]{1,0:T(8,128)(2,1)S(1)} %get-tuple-element.17.refs_3_), channel_id=1, source_target_pairs={{0,16},{8,24},{16,32},{24,40},{32,48},{40,56},{48,0},{56,8},{64,80... | collective-permute-start | bytes 393224 | tf_op jit(solution)/shard_map/ppermute | solution.py:52
  31.6 0.0 collective-permute-start.10
  31.6 0.1 pad_add_fusion.place_ref
  32.4 1.2 %prepare.1 = (bf16[512,256]{1,0:T(8,128)(2,1)S(1)}, bf16[512,256]{1,0:T(8,128)(2,1)S(1)}, bf16[256,128]{1,0:T(8,128)(2,1)S(1)}, bf16[256,256]{1,0:T(8,128)(2,1)S(1)}, f32[256,128]{1,0:T(8,128)S(1)}) custom-call(s32[2]{0:T(128)S(1)} %pad_add_fusion.place_ref, f32[1]{0:T(128)S(6)} %copy.7.damp_ref, f32[64,128]{1,0:T(8,128)S(1)} %join.8.refs_0_, ...), custom_call_target="tpu_custom_call" | custom-call | flops 200000000 | bytes 1048576 | tf_op jit(solution)/shard_map/prepare/pallas_call | solution.py:183
  33.6 0.0 copy-start
  33.6 0.9 %copy-done = bf16[1,32,4096]{2,1,0:T(8,128)(2,1)S(1)} copy-done((bf16[1,32,4096]{2,1,0:T(8,128)(2,1)S(1)}, bf16[1,32,4096]{2,1,0:T(8,128)(2,1)}, u32[]{:S(2)}) %copy-start) | copy-done | bytes 262168
  34.5 2.6 %rotate.2.refs_2_.refs_0_ = bf16[96,4096]{1,0:T(8,128)(2,1)S(1)} custom-call(bf16[512,256]{1,0:T(8,128)(2,1)S(1)} %get-tuple-element.12.left_ref, bf16[512,256]{1,0:T(8,128)(2,1)S(1)} %get-tuple-element.13.right_ref, bf16[256,128]{1,0:T(8,128)(2,1)S(1)} %get-tuple-element.14.in_ref, bf16[256,256]{1,0:T(8,128)(2,1)S(1)} %get-tuple-element.15.back_ref, ...), custom_call_target="tpu_custom_call" | custom-call | tf_op jit(solution)/shard_map/rotate/pallas_call | solution.py:252
  37.1 0.3 collective-permute-start.13
  37.4 1.8 %collective-permute-start.14 = (bf16[96,4096]{1,0:T(8,128)(2,1)S(1)}, bf16[96,4096]{1,0:T(8,128)(2,1)S(1)}, u32[]{:S(2)}, u32[]{:S(2)}) collective-permute-start(bf16[96,4096]{1,0:T(8,128)(2,1)S(1)} %rotate.2.refs_2_.refs_0_), channel_id=1, source_target_pairs={{0,192},{8,200},{16,208},{24,216},{32,224},{40,232},{48,240},{56,2... | collective-permute-start | bytes 2359304 | tf_op jit(solution)/shard_map/ppermute | solution.py:52
  39.2 1.4 %rotate.3.refs_0_.refs_1_ = bf16[32,4096]{1,0:T(8,128)(2,1)S(1)} custom-call(bf16[512,256]{1,0:T(8,128)(2,1)S(1)} %get-tuple-element.12.left_ref, bf16[512,256]{1,0:T(8,128)(2,1)S(1)} %get-tuple-element.13.right_ref, bf16[256,128]{1,0:T(8,128)(2,1)S(1)} %get-tuple-element.14.in_ref, bf16[256,256]{1,0:T(8,128)(2,1)S(1)} %get-tuple-element.15.back_ref, ...), custom_call_target="tpu_custom_call" | custom-call | flops 20000000000 | tf_op jit(solution)/shard_map/rotate/pallas_call | solution.py:252
  40.6 1.6 %collective-permute-start.15 = (bf16[32,4096]{1,0:T(8,128)(2,1)S(1)}, bf16[32,4096]{1,0:T(8,128)(2,1)S(1)}, u32[]{:S(2)}, u32[]{:S(2)}) collective-permute-start(bf16[32,4096]{1,0:T(8,128)(2,1)S(1)} %rotate.3.refs_0_.refs_1_), channel_id=1, source_target_pairs={{0,64},{8,72},{16,80},{24,88},{32,96},{40,104},{48,112},{56,120},{... | collective-permute-start | bytes 786440 | tf_op jit(solution)/shard_map/ppermute | solution.py:52
  42.2 0.5 collective-permute-start.16
  42.7 2.2 %held.1.refs_2_ = bf16[512,4096]{1,0:T(8,128)(2,1)S(1)} custom-call(bf16[512,4096]{1,0:T(8,128)(2,1)} %collective-permute-done.11.x_ref, bf16[32,4096]{1,0:T(8,128)(2,1)S(1)} %rotate.3.refs_0_.refs_1_), custom_call_target="tpu_custom_call" | custom-call | bytes 8388608 | tf_op jit(solution)/shard_map/held/pallas_call | solution.py:73
  44.9 0.1 join.9
  45.0 0.0 copy-start.4
  45.0 1.6 %convolution_convert_fusion.4 = bf16[128,512]{1,0:T(8,128)(2,1)S(1)} fusion(bf16[128,4096]{1,0:T(8,128)(2,1)S(1)} %join.9, bf16[512,4096]{1,0:T(8,128)(2,1)S(1)} %held.1.refs_2_), kind=kOutput, calls=%fused_computation.4 | convolution fusion | flops 536936448 | bytes 5373952 | tf_op jit(solution)/shard_map/dot_general | solution.py:264
  46.6 0.1 collective-permute-start.12
  46.7 0.5 copy-done.4
  47.2 1.5 %convolution_convert_fusion.5.refs_2_.refs_1_.refs_0_ = bf16[128,512]{1,0:T(8,128)(2,1)S(1)} fusion(bf16[128,4096]{1,0:T(8,128)(2,1)S(1)} %join.9, bf16[1,512,4096]{2,1,0:T(8,128)(2,1)S(1)} %copy-done.4), kind=kOutput, calls=%fused_computation.5 | convolution fusion | flops 536936448 | bytes 5373952 | tf_op jit(solution)/shard_map/dot_general | solution.py:264
  48.7 11.7 %collective-permute-done.15.refs_1_.refs_2_ = bf16[32,4096]{1,0:T(8,128)(2,1)S(1)} collective-permute-done((bf16[32,4096]{1,0:T(8,128)(2,1)S(1)}, bf16[32,4096]{1,0:T(8,128)(2,1)S(1)}, u32[]{:S(2)}, u32[]{:S(2)}) %collective-permute-start.15) | collective-permute-done | bytes 262176 | tf_op jit(solution)/shard_map/ppermute | solution.py:52
  60.4 0.4 collective-permute-start.18
  60.9 1.8 %collective-permute-start.19 = (bf16[64,4096]{1,0:T(8,128)(2,1)S(1)}, bf16[64,4096]{1,0:T(8,128)(2,1)S(1)}, u32[]{:S(2)}, u32[]{:S(2)}) collective-permute-start(bf16[64,4096]{1,0:T(8,128)(2,1)S(1)} %join.11.refs_5_), channel_id=1, source_target_pairs={{0,192},{8,200},{16,208},{24,216},{32,224},{40,232},{48,240},{56,2... | collective-permute-start | bytes 1572872 | tf_op jit(solution)/shard_map/ppermute | solution.py:52
  62.7 0.1 join.12
  62.8 1.3 %convolution_convert_fusion = bf16[256,512]{1,0:T(8,128)(2,1)S(1)} fusion(bf16[256,4096]{1,0:T(8,128)(2,1)S(1)} %join.12, bf16[512,4096]{1,0:T(8,128)(2,1)S(1)} %held.1.refs_2_), kind=kOutput, calls=%fused_computation | convolution fusion | flops 1073872896 | bytes 6553600 | tf_op jit(solution)/shard_map/dot_general | solution.py:264
  64.1 0.1 collective-permute-start.17
  64.2 1.3 %convolution_convert_fusion.1.refs_2_ = bf16[256,512]{1,0:T(8,128)(2,1)S(1)} fusion(bf16[256,4096]{1,0:T(8,128)(2,1)S(1)} %join.12, bf16[1,512,4096]{2,1,0:T(8,128)(2,1)S(1)} %copy-done.4), kind=kOutput, calls=%fused_computation.1 | convolution fusion | flops 1073872896 | bytes 6553600 | tf_op jit(solution)/shard_map/dot_general | solution.py:264
  65.5 4.9 %collective-permute-done.18.refs_0_ = bf16[64,4096]{1,0:T(8,128)(2,1)S(1)} collective-permute-done((bf16[64,4096]{1,0:T(8,128)(2,1)S(1)}, bf16[64,4096]{1,0:T(8,128)(2,1)S(1)}, u32[]{:S(2)}, u32[]{:S(2)}) %collective-permute-start.18) | collective-permute-done | bytes 524320 | tf_op jit(solution)/shard_map/ppermute | solution.py:52
  70.4 1.5 %collective-permute-done.19.refs_1_ = bf16[64,4096]{1,0:T(8,128)(2,1)S(1)} collective-permute-done((bf16[64,4096]{1,0:T(8,128)(2,1)S(1)}, bf16[64,4096]{1,0:T(8,128)(2,1)S(1)}, u32[]{:S(2)}, u32[]{:S(2)}) %collective-permute-start.19) | collective-permute-done | bytes 524320 | tf_op jit(solution)/shard_map/ppermute | solution.py:52
  71.9 0.1 join.13
  72.0 1.6 %convolution_convert_fusion.2 = bf16[128,512]{1,0:T(8,128)(2,1)S(1)} fusion(bf16[128,4096]{1,0:T(8,128)(2,1)S(1)} %join.13, bf16[512,4096]{1,0:T(8,128)(2,1)S(1)} %held.1.refs_2_), kind=kOutput, calls=%fused_computation.2 | convolution fusion | flops 536936448 | bytes 5373952 | tf_op jit(solution)/shard_map/dot_general | solution.py:264
  73.6 0.3 collective-permute-start.20
  73.9 1.5 %convolution_convert_fusion.3.refs_4_ = bf16[128,512]{1,0:T(8,128)(2,1)S(1)} fusion(bf16[128,4096]{1,0:T(8,128)(2,1)S(1)} %join.13, bf16[1,512,4096]{2,1,0:T(8,128)(2,1)S(1)} %copy-done.4), kind=kOutput, calls=%fused_computation.3 | convolution fusion | flops 536936448 | bytes 5373952 | tf_op jit(solution)/shard_map/dot_general | solution.py:264
  75.5 0.7 arrange.1
  76.2 1.6 %collective-permute-start.24 = (bf16[2,128,512]{2,1,0:T(8,128)(2,1)S(1)}, bf16[2,128,512]{2,1,0:T(8,128)(2,1)S(1)}, u32[]{:S(2)}, u32[]{:S(2)}) collective-permute-start(bf16[2,128,512]{2,1,0:T(8,128)(2,1)S(1)} %bitcast.44), channel_id=1, source_target_pairs={{0,1},{1,2},{2,3},{3,0},{4,5},{5,6},{6,7},{7,4},{8,11},{9,8},{10,9... | collective-permute-start | bytes 786440 | tf_op jit(solution)/shard_map/ppermute | solution.py:48
  77.9 1.2 %collective-permute-start.21 = (bf16[128,512]{1,0:T(8,128)(2,1)S(1)}, bf16[128,512]{1,0:T(8,128)(2,1)S(1)}, u32[]{:S(2)}, u32[]{:S(2)}) collective-permute-start(bf16[128,512]{1,0:T(8,128)(2,1)S(1)} %bitcast.47), channel_id=1, source_target_pairs={{0,4},{1,5},{2,6},{3,7},{4,0},{5,1},{6,2},{7,3},{8,12},{9,13},{10,... | collective-permute-start | bytes 393224 | tf_op jit(solution)/shard_map/ppermute | solution.py:48
  79.1 1.7 %collective-permute-start.22 = (bf16[128,512]{1,0:T(8,128)(2,1)S(1)}, bf16[128,512]{1,0:T(8,128)(2,1)S(1)}, u32[]{:S(2)}, u32[]{:S(2)}) collective-permute-start(bf16[128,512]{1,0:T(8,128)(2,1)S(1)} %bitcast.46), channel_id=1, source_target_pairs={{0,3},{1,0},{2,1},{3,2},{4,7},{5,4},{6,5},{7,6},{8,9},{9,10},{10,1... | collective-permute-start | bytes 393224 | tf_op jit(solution)/shard_map/ppermute | solution.py:48
  80.8 1.9 %collective-permute-start.23 = (bf16[128,512]{1,0:T(8,128)(2,1)S(1)}, bf16[128,512]{1,0:T(8,128)(2,1)S(1)}, u32[]{:S(2)}, u32[]{:S(2)}) collective-permute-start(bf16[128,512]{1,0:T(8,128)(2,1)S(1)} %bitcast.45), channel_id=1, source_target_pairs={{0,7},{1,4},{2,5},{3,6},{4,3},{5,0},{6,1},{7,2},{8,13},{9,14},{10,... | collective-permute-start | bytes 393224 | tf_op jit(solution)/shard_map/ppermute | solution.py:48
  82.7 1.2 %collective-permute-done.24 = bf16[2,128,512]{2,1,0:T(8,128)(2,1)S(1)} collective-permute-done((bf16[2,128,512]{2,1,0:T(8,128)(2,1)S(1)}, bf16[2,128,512]{2,1,0:T(8,128)(2,1)S(1)}, u32[]{:S(2)}, u32[]{:S(2)}) %collective-permute-start.24) | collective-permute-done | bytes 262176 | tf_op jit(solution)/shard_map/ppermute | solution.py:48
  83.9 0.1 fusion
  84.0 2.2 %collective-permute-start.25 = (bf16[128,512]{1,0:T(8,128)(2,1)S(1)}, bf16[128,512]{1,0:T(8,128)(2,1)S(1)}, u32[]{:S(2)}, u32[]{:S(2)}) collective-permute-start(bf16[128,512]{1,0:T(8,128)(2,1)S(1)} %get-tuple-element.26), channel_id=1, source_target_pairs={{0,1},{1,2},{2,3},{3,0},{4,5},{5,6},{6,7},{7,4},{8,11},{9,8},{10,9... | collective-permute-start | bytes 393224 | tf_op jit(solution)/shard_map/ppermute | solution.py:48
  86.2 3.0 %collective-permute-start.26 = (bf16[128,512]{1,0:T(8,128)(2,1)S(1)}, bf16[128,512]{1,0:T(8,128)(2,1)S(1)}, u32[]{:S(2)}, u32[]{:S(2)}) collective-permute-start(bf16[128,512]{1,0:T(8,128)(2,1)S(1)} %get-tuple-element.25), channel_id=1, source_target_pairs={{0,5},{1,6},{2,7},{3,4},{4,1},{5,2},{6,3},{7,0},{8,15},{9,12},{10,... | collective-permute-start | bytes 393224 | tf_op jit(solution)/shard_map/ppermute | solution.py:48
  89.2 1.0 %collective-permute-done.25.refs_4_ = bf16[128,512]{1,0:T(8,128)(2,1)S(1)} collective-permute-done((bf16[128,512]{1,0:T(8,128)(2,1)S(1)}, bf16[128,512]{1,0:T(8,128)(2,1)S(1)}, u32[]{:S(2)}, u32[]{:S(2)}) %collective-permute-start.25) | collective-permute-done | bytes 131104 | tf_op jit(solution)/shard_map/ppermute | solution.py:48
  90.3 3.0 %collective-permute-done.26.refs_5_ = bf16[128,512]{1,0:T(8,128)(2,1)S(1)} collective-permute-done((bf16[128,512]{1,0:T(8,128)(2,1)S(1)}, bf16[128,512]{1,0:T(8,128)(2,1)S(1)}, u32[]{:S(2)}, u32[]{:S(2)}) %collective-permute-start.26) | collective-permute-done | bytes 131104 | tf_op jit(solution)/shard_map/ppermute | solution.py:48
  93.3 0.8 finish.1
  (26 shorter events, 0.3 us)
Async XLA Ops:
  0.0 42.7 %collective-permute-start.11 = (bf16[512,4096]{1,0:T(8,128)(2,1)}, bf16[512,4096]{1,0:T(8,128)(2,1)}, u32[]{:S(2)}, u32[]{:S(2)}) collective-permute-start(bf16[512,4096]{1,0:T(8,128)(2,1)} %bitcast.42), channel_id=1, source_target_pairs={{0,8},{8,0},{16,24},{24,16},{32,40},{40,32},{48,56},{56,48},{64,72... | collective-permute-start | bytes 12582920 | tf_op jit(solution)/shard_map/ppermute | solution.py:52
  0.0 27.4 %collective-permute-start.7 = (bf16[32,4096]{1,0:T(8,128)(2,1)}, bf16[32,4096]{1,0:T(8,128)(2,1)S(1)}, u32[]{:S(2)}, u32[]{:S(2)}) collective-permute-start(bf16[32,4096]{1,0:T(8,128)(2,1)} %bitcast.36), channel_id=1, source_target_pairs={{0,16},{8,24},{16,32},{24,40},{32,48},{40,56},{48,0},{56,8},{64,80... | collective-permute-start | bytes 786440 | tf_op jit(solution)/shard_map/ppermute | solution.py:52
  3.3 24.1 %collective-permute-start.8 = (bf16[32,4096]{1,0:T(8,128)(2,1)}, bf16[32,4096]{1,0:T(8,128)(2,1)S(1)}, u32[]{:S(2)}, u32[]{:S(2)}) collective-permute-start(bf16[32,4096]{1,0:T(8,128)(2,1)} %bitcast.37), channel_id=1, source_target_pairs={{0,48},{8,56},{16,0},{24,8},{32,16},{40,24},{48,32},{56,40},{64,11... | collective-permute-start | bytes 786440 | tf_op jit(solution)/shard_map/ppermute | solution.py:52
  6.4 0.7 copy-start.1
  7.1 0.7 copy-start.2
  7.7 0.7 copy-start.3
  8.4 1.3 %collective-permute-start = (f32[8,128]{1,0:T(8,128)S(1)}, f32[8,128]{1,0:T(8,128)S(1)}, u32[]{:S(2)}, u32[]{:S(2)}) collective-permute-start(f32[8,128]{1,0:T(8,128)S(1)} %pack.1.refs_0_), channel_id=1, source_target_pairs={{0,8},{8,0},{16,24},{24,16},{32,40},{40,32},{48,56},{56,48},{64,72... | collective-permute-start | bytes 12296 | tf_op jit(solution)/shard_map/ppermute | solution.py:52
  9.7 3.7 %collective-permute-start.1 = (f32[16,128]{1,0:T(8,128)S(1)}, f32[16,128]{1,0:T(8,128)S(1)}, u32[]{:S(2)}, u32[]{:S(2)}) collective-permute-start(f32[16,128]{1,0:T(8,128)S(1)} %join.7.refs_0_), channel_id=1, source_target_pairs={{0,64},{8,72},{16,80},{24,88},{32,96},{40,104},{48,112},{56,120},{... | collective-permute-start | bytes 24584 | tf_op jit(solution)/shard_map/ppermute | solution.py:52
  9.9 5.2 %collective-permute-start.2 = (f32[16,128]{1,0:T(8,128)S(1)}, f32[16,128]{1,0:T(8,128)S(1)}, u32[]{:S(2)}, u32[]{:S(2)}) collective-permute-start(f32[16,128]{1,0:T(8,128)S(1)} %join.7.refs_0_), channel_id=1, source_target_pairs={{0,128},{8,136},{16,144},{24,152},{32,160},{40,168},{48,176},{56,1... | collective-permute-start | bytes 24584 | tf_op jit(solution)/shard_map/ppermute | solution.py:52
  13.3 4.9 %collective-permute-start.3 = (f32[16,128]{1,0:T(8,128)S(1)}, f32[16,128]{1,0:T(8,128)S(1)}, u32[]{:S(2)}, u32[]{:S(2)}) collective-permute-start(f32[16,128]{1,0:T(8,128)S(1)} %join.7.refs_0_), channel_id=1, source_target_pairs={{0,192},{8,200},{16,208},{24,216},{32,224},{40,232},{48,240},{56,2... | collective-permute-start | bytes 24584 | tf_op jit(solution)/shard_map/ppermute | solution.py:52
  18.2 6.2 %collective-permute-start.4 = (f32[64,128]{1,0:T(8,128)S(1)}, f32[64,128]{1,0:T(8,128)S(1)}, u32[]{:S(2)}, u32[]{:S(2)}) collective-permute-start(f32[64,128]{1,0:T(8,128)S(1)} %join.8.refs_0_), channel_id=1, source_target_pairs={{0,16},{8,24},{16,32},{24,40},{32,48},{40,56},{48,0},{56,8},{64,80... | collective-permute-start | bytes 98312 | tf_op jit(solution)/shard_map/ppermute | solution.py:52
  19.6 7.8 %collective-permute-start.5 = (f32[64,128]{1,0:T(8,128)S(1)}, f32[64,128]{1,0:T(8,128)S(1)}, u32[]{:S(2)}, u32[]{:S(2)}) collective-permute-start(f32[64,128]{1,0:T(8,128)S(1)} %join.8.refs_0_), channel_id=1, source_target_pairs={{0,32},{8,40},{16,48},{24,56},{32,0},{40,8},{48,16},{56,24},{64,96... | collective-permute-start | bytes 98312 | tf_op jit(solution)/shard_map/ppermute | solution.py:52
  24.4 8.0 %collective-permute-start.6 = (f32[64,128]{1,0:T(8,128)S(1)}, f32[64,128]{1,0:T(8,128)S(1)}, u32[]{:S(2)}, u32[]{:S(2)}) collective-permute-start(f32[64,128]{1,0:T(8,128)S(1)} %join.8.refs_0_), channel_id=1, source_target_pairs={{0,48},{8,56},{16,0},{24,8},{32,16},{40,24},{48,32},{56,40},{64,11... | collective-permute-start | bytes 98312 | tf_op jit(solution)/shard_map/ppermute | solution.py:52
  27.4 11.8 %collective-permute-start.9 = (bf16[16,4096]{1,0:T(8,128)(2,1)S(1)}, bf16[16,4096]{1,0:T(8,128)(2,1)S(1)}, u32[]{:S(2)}, u32[]{:S(2)}) collective-permute-start(bf16[16,4096]{1,0:T(8,128)(2,1)S(1)} %get-tuple-element.17.refs_3_), channel_id=1, source_target_pairs={{0,16},{8,24},{16,32},{24,40},{32,48},{40,56},{48,0},{56,8},{64,80... | collective-permute-start | bytes 393224 | tf_op jit(solution)/shard_map/ppermute | solution.py:52
  31.6 7.6 %collective-permute-start.10 = (bf16[16,4096]{1,0:T(8,128)(2,1)S(1)}, bf16[16,4096]{1,0:T(8,128)(2,1)S(1)}, u32[]{:S(2)}, u32[]{:S(2)}) collective-permute-start(bf16[16,4096]{1,0:T(8,128)(2,1)S(1)} %get-tuple-element.18), channel_id=1, source_target_pairs={{0,48},{8,56},{16,0},{24,8},{32,16},{40,24},{48,32},{56,40},{64,11... | collective-permute-start | bytes 393224 | tf_op jit(solution)/shard_map/ppermute | solution.py:52
  33.6 1.0 %copy-start = (bf16[1,32,4096]{2,1,0:T(8,128)(2,1)S(1)}, bf16[1,32,4096]{2,1,0:T(8,128)(2,1)}, u32[]{:S(2)}) copy-start(bf16[1,32,4096]{2,1,0:T(8,128)(2,1)} %param.6) | copy-start | bytes 786436
  37.1 23.3 %collective-permute-start.13 = (bf16[96,4096]{1,0:T(8,128)(2,1)S(1)}, bf16[96,4096]{1,0:T(8,128)(2,1)S(1)}, u32[]{:S(2)}, u32[]{:S(2)}) collective-permute-start(bf16[96,4096]{1,0:T(8,128)(2,1)S(1)} %rotate.2.refs_2_.refs_0_), channel_id=1, source_target_pairs={{0,64},{8,72},{16,80},{24,88},{32,96},{40,104},{48,112},{56,120},{... | collective-permute-start | bytes 2359304 | tf_op jit(solution)/shard_map/ppermute | solution.py:52
  37.4 23.4 %collective-permute-start.14 = (bf16[96,4096]{1,0:T(8,128)(2,1)S(1)}, bf16[96,4096]{1,0:T(8,128)(2,1)S(1)}, u32[]{:S(2)}, u32[]{:S(2)}) collective-permute-start(bf16[96,4096]{1,0:T(8,128)(2,1)S(1)} %rotate.2.refs_2_.refs_0_), channel_id=1, source_target_pairs={{0,192},{8,200},{16,208},{24,216},{32,224},{40,232},{48,240},{56,2... | collective-permute-start | bytes 2359304 | tf_op jit(solution)/shard_map/ppermute | solution.py:52
  40.6 19.8 %collective-permute-start.15 = (bf16[32,4096]{1,0:T(8,128)(2,1)S(1)}, bf16[32,4096]{1,0:T(8,128)(2,1)S(1)}, u32[]{:S(2)}, u32[]{:S(2)}) collective-permute-start(bf16[32,4096]{1,0:T(8,128)(2,1)S(1)} %rotate.3.refs_0_.refs_1_), channel_id=1, source_target_pairs={{0,64},{8,72},{16,80},{24,88},{32,96},{40,104},{48,112},{56,120},{... | collective-permute-start | bytes 786440 | tf_op jit(solution)/shard_map/ppermute | solution.py:52
  42.2 20.5 %collective-permute-start.16 = (bf16[32,4096]{1,0:T(8,128)(2,1)S(1)}, bf16[32,4096]{1,0:T(8,128)(2,1)S(1)}, u32[]{:S(2)}, u32[]{:S(2)}) collective-permute-start(bf16[32,4096]{1,0:T(8,128)(2,1)S(1)} %rotate.3.refs_0_.refs_1_), channel_id=1, source_target_pairs={{0,192},{8,200},{16,208},{24,216},{32,224},{40,232},{48,240},{56,2... | collective-permute-start | bytes 786440 | tf_op jit(solution)/shard_map/ppermute | solution.py:52
  45.0 2.2 %copy-start.4 = (bf16[1,512,4096]{2,1,0:T(8,128)(2,1)S(1)}, bf16[1,512,4096]{2,1,0:T(8,128)(2,1)}, u32[]{:S(2)}) copy-start(bf16[1,512,4096]{2,1,0:T(8,128)(2,1)} %param.7) | copy-start | bytes 12582916
  46.6 28.8 %collective-permute-start.12 = (bf16[128,512]{1,0:T(8,128)(2,1)S(1)}, bf16[128,512]{1,0:T(8,128)(2,1)S(1)}, u32[]{:S(2)}, u32[]{:S(2)}) collective-permute-start(bf16[128,512]{1,0:T(8,128)(2,1)S(1)} %convolution_convert_fusion.4), channel_id=1, source_target_pairs={{0,8},{8,0},{16,24},{24,16},{32,40},{40,32},{48,56},{56,48},{64,72... | collective-permute-start | bytes 393224 | tf_op jit(solution)/shard_map/ppermute | solution.py:52
  60.4 10.0 %collective-permute-start.18 = (bf16[64,4096]{1,0:T(8,128)(2,1)S(1)}, bf16[64,4096]{1,0:T(8,128)(2,1)S(1)}, u32[]{:S(2)}, u32[]{:S(2)}) collective-permute-start(bf16[64,4096]{1,0:T(8,128)(2,1)S(1)} %join.10.refs_4_), channel_id=1, source_target_pairs={{0,64},{8,72},{16,80},{24,88},{32,96},{40,104},{48,112},{56,120},{... | collective-permute-start | bytes 1572872 | tf_op jit(solution)/shard_map/ppermute | solution.py:52
  60.9 11.1 %collective-permute-start.19 = (bf16[64,4096]{1,0:T(8,128)(2,1)S(1)}, bf16[64,4096]{1,0:T(8,128)(2,1)S(1)}, u32[]{:S(2)}, u32[]{:S(2)}) collective-permute-start(bf16[64,4096]{1,0:T(8,128)(2,1)S(1)} %join.11.refs_5_), channel_id=1, source_target_pairs={{0,192},{8,200},{16,208},{24,216},{32,224},{40,232},{48,240},{56,2... | collective-permute-start | bytes 1572872 | tf_op jit(solution)/shard_map/ppermute | solution.py:52
  64.1 11.3 %collective-permute-start.17 = (bf16[256,512]{1,0:T(8,128)(2,1)S(1)}, bf16[256,512]{1,0:T(8,128)(2,1)S(1)}, u32[]{:S(2)}, u32[]{:S(2)}) collective-permute-start(bf16[256,512]{1,0:T(8,128)(2,1)S(1)} %convolution_convert_fusion), channel_id=1, source_target_pairs={{0,8},{8,0},{16,24},{24,16},{32,40},{40,32},{48,56},{56,48},{64,72... | collective-permute-start | bytes 786440 | tf_op jit(solution)/shard_map/ppermute | solution.py:52
  73.6 1.9 %collective-permute-start.20 = (bf16[128,512]{1,0:T(8,128)(2,1)S(1)}, bf16[128,512]{1,0:T(8,128)(2,1)S(1)}, u32[]{:S(2)}, u32[]{:S(2)}) collective-permute-start(bf16[128,512]{1,0:T(8,128)(2,1)S(1)} %convolution_convert_fusion.2), channel_id=1, source_target_pairs={{0,8},{8,0},{16,24},{24,16},{32,40},{40,32},{48,56},{56,48},{64,72... | collective-permute-start | bytes 393224 | tf_op jit(solution)/shard_map/ppermute | solution.py:52
  76.2 7.7 %collective-permute-start.24 = (bf16[2,128,512]{2,1,0:T(8,128)(2,1)S(1)}, bf16[2,128,512]{2,1,0:T(8,128)(2,1)S(1)}, u32[]{:S(2)}, u32[]{:S(2)}) collective-permute-start(bf16[2,128,512]{2,1,0:T(8,128)(2,1)S(1)} %bitcast.44), channel_id=1, source_target_pairs={{0,1},{1,2},{2,3},{3,0},{4,5},{5,6},{6,7},{7,4},{8,11},{9,8},{10,9... | collective-permute-start | bytes 786440 | tf_op jit(solution)/shard_map/ppermute | solution.py:48
  77.9 11.4 %collective-permute-start.21 = (bf16[128,512]{1,0:T(8,128)(2,1)S(1)}, bf16[128,512]{1,0:T(8,128)(2,1)S(1)}, u32[]{:S(2)}, u32[]{:S(2)}) collective-permute-start(bf16[128,512]{1,0:T(8,128)(2,1)S(1)} %bitcast.47), channel_id=1, source_target_pairs={{0,4},{1,5},{2,6},{3,7},{4,0},{5,1},{6,2},{7,3},{8,12},{9,13},{10,... | collective-permute-start | bytes 393224 | tf_op jit(solution)/shard_map/ppermute | solution.py:48
  79.1 10.2 %collective-permute-start.22 = (bf16[128,512]{1,0:T(8,128)(2,1)S(1)}, bf16[128,512]{1,0:T(8,128)(2,1)S(1)}, u32[]{:S(2)}, u32[]{:S(2)}) collective-permute-start(bf16[128,512]{1,0:T(8,128)(2,1)S(1)} %bitcast.46), channel_id=1, source_target_pairs={{0,3},{1,0},{2,1},{3,2},{4,7},{5,4},{6,5},{7,6},{8,9},{9,10},{10,1... | collective-permute-start | bytes 393224 | tf_op jit(solution)/shard_map/ppermute | solution.py:48
  80.8 8.4 %collective-permute-start.23 = (bf16[128,512]{1,0:T(8,128)(2,1)S(1)}, bf16[128,512]{1,0:T(8,128)(2,1)S(1)}, u32[]{:S(2)}, u32[]{:S(2)}) collective-permute-start(bf16[128,512]{1,0:T(8,128)(2,1)S(1)} %bitcast.45), channel_id=1, source_target_pairs={{0,7},{1,4},{2,5},{3,6},{4,3},{5,0},{6,1},{7,2},{8,13},{9,14},{10,... | collective-permute-start | bytes 393224 | tf_op jit(solution)/shard_map/ppermute | solution.py:48
  84.0 6.3 %collective-permute-start.25 = (bf16[128,512]{1,0:T(8,128)(2,1)S(1)}, bf16[128,512]{1,0:T(8,128)(2,1)S(1)}, u32[]{:S(2)}, u32[]{:S(2)}) collective-permute-start(bf16[128,512]{1,0:T(8,128)(2,1)S(1)} %get-tuple-element.26), channel_id=1, source_target_pairs={{0,1},{1,2},{2,3},{3,0},{4,5},{5,6},{6,7},{7,4},{8,11},{9,8},{10,9... | collective-permute-start | bytes 393224 | tf_op jit(solution)/shard_map/ppermute | solution.py:48
  86.2 7.1 %collective-permute-start.26 = (bf16[128,512]{1,0:T(8,128)(2,1)S(1)}, bf16[128,512]{1,0:T(8,128)(2,1)S(1)}, u32[]{:S(2)}, u32[]{:S(2)}) collective-permute-start(bf16[128,512]{1,0:T(8,128)(2,1)S(1)} %get-tuple-element.25), channel_id=1, source_target_pairs={{0,5},{1,6},{2,7},{3,4},{4,1},{5,2},{6,3},{7,0},{8,15},{9,12},{10,... | collective-permute-start | bytes 393224 | tf_op jit(solution)/shard_map/ppermute | solution.py:48
